TPU v7x, 768 devices: a whole 4x8x12 slice. The times are simulated.
768 devices in a mesh: dst: 64 (over x, y, core), src: 12 (over z).
Axes of the slice: x: 4, y: 8, z: 12, core: 2. Of those that a mesh axis runs over, the one named last changes fastest.
Arguments:
- node_hidden_state: bfloat16 [24576, 256], P(('dst', 'src')), may hold values from -6 to 6
- self_projection_weight: bfloat16 [256, 256], replicated, may hold values from -0.375 to 0.375
- weight_value: bfloat16 [256, 256], replicated, may hold values from -0.375 to 0.375
- weight_edge: bfloat16 [256, 8], replicated, may hold values from -0.375 to 0.375
- weight_target: bfloat16 [256, 8], replicated, may hold values from -0.375 to 0.375
- layer_norm_gain: float32 [256], replicated, may hold values from 0.25 to 1.75
- edge_scale: float32 [8], replicated, may hold values from 0.5 to 2
- tile_index: int32 [64, 12, 8, 2], P('dst', 'src'), may hold values from 0 to 15, as said below
- tile_count: int32 [64, 12], P('dst', 'src'), may hold values from 2 to 8, as said below
- edge_feature: bfloat16 [64, 12, 8, 8, 128, 128], P('dst', 'src'), may hold values from -6 to 6
- edge_mask: int32 [64, 12, 8, 128, 128], P('dst', 'src'), may hold values from 0 to 1, as said below
- cotangent: bfloat16 [24576, 256], P(('dst', 'src')), may hold values from -6 to 6
Outputs:
- updated_node_features: bfloat16 [24576, 256], P(('dst', 'src'))
- node_grad: float32 [24576, 256], P(('dst', 'src'))
- edge_grad: bfloat16 [64, 12, 8, 8, 128, 128], P('dst', 'src')
Inputs may be any that keep to these rules, and one draw needn't show every extreme that they name: `tile_index`: within one device's slots the pairs are distinct; the first entry is a row block below 3, the second a column block below 16; slots at or after the device's tile_count are padding. `tile_count`: number of live slots of each device; some device has all 8 live. `edge_mask`: some destination nodes have no edges in any tile.
All inputs are finite; a program needn't handle non-finite values.
Results may differ from a plain program's by a relative error of at most 0.0065.
Values may be sent and summed in bfloat16 or wider, within the bound.
A program may use at most 32 MiB of HBM per device.

v0:
```python
import jax
import jax.numpy as jnp
from jax import lax
from jax.sharding import PartitionSpec as P


def node_update_forward(
    state, numerator_total, denominator_total, self_projection_weight, layer_norm_gain, head_count
):
    count = state.shape[0]
    denominator_floor = denominator_total + 1.0
    agg = (numerator_total.reshape(count, head_count, -1) / denominator_floor[:, :, None]).reshape(
        count, -1
    )
    pre = jnp.dot(state, self_projection_weight, preferred_element_type=jnp.float32) + agg
    centred_values = pre - jnp.mean(pre, axis=-1, keepdims=True)
    inverse_scale = lax.rsqrt(
        jnp.mean(centred_values * centred_values, axis=-1, keepdims=True) + 1e-05
    )
    normalized_input = centred_values * inverse_scale
    normed_output = normalized_input * layer_norm_gain
    updated_node_features = (state.astype(jnp.float32) + jax.nn.silu(normed_output)).astype(
        jnp.bfloat16
    )
    return (
        updated_node_features,
        denominator_floor,
        normalized_input,
        inverse_scale,
        normed_output,
    )


def node_update_backward(
    cotangent,
    normed_output,
    normalized_input,
    inverse_scale,
    layer_norm_gain,
    numerator_total,
    denominator_floor,
    head_count,
):
    count = cotangent.shape[0]
    logistic = jax.nn.sigmoid(normed_output)
    grad_y = cotangent.astype(jnp.float32) * logistic * (1.0 + normed_output * (1.0 - logistic))
    normed_input_gradient = grad_y * layer_norm_gain
    preactivation_gradient = inverse_scale * (
        normed_input_gradient
        - jnp.mean(normed_input_gradient, axis=-1, keepdims=True)
        - normalized_input
        * jnp.mean(normed_input_gradient * normalized_input, axis=-1, keepdims=True)
    )
    numerator_gradient = (
        (preactivation_gradient.reshape(count, head_count, -1) / denominator_floor[:, :, None])
        .reshape(count, -1)
        .astype(jnp.bfloat16)
    )
    inner = jnp.sum(
        (preactivation_gradient * numerator_total).reshape(count, head_count, -1), axis=-1
    )
    denominator_gradient = (-inner / (denominator_floor * denominator_floor)).astype(jnp.bfloat16)
    return (preactivation_gradient, numerator_gradient, denominator_gradient)


def body(
    node_hidden_state,
    self_projection_weight,
    weight_value,
    weight_edge,
    weight_target,
    layer_norm_gain,
    edge_scale,
    tile_index,
    tile_count,
    edge_feature,
    edge_mask,
    cotangent,
):
    f32 = jnp.float32
    low = jnp.bfloat16
    head_count = edge_scale.shape[0]
    width = node_hidden_state.shape[1]
    size_head = width // head_count
    block = edge_mask.shape[-1]
    slots = edge_mask.shape[2]
    owned = node_hidden_state.shape[0]
    zero = jnp.zeros((), jnp.int32)
    value = jnp.dot(node_hidden_state, weight_value, preferred_element_type=f32).astype(low)
    source_gate = jnp.dot(node_hidden_state, weight_edge, preferred_element_type=f32).astype(low)
    target_gate = jnp.dot(node_hidden_state, weight_target, preferred_element_type=f32).astype(low)
    value_all, gate_all = (
        lax.all_gather(value, "dst", axis=0, tiled=True),
        lax.all_gather(source_gate, "dst", axis=0, tiled=True),
    )
    target_all = lax.all_gather(target_gate, "src", axis=0, tiled=True)
    group_rows = value_all.shape[0]
    dest_rows = owned * lax.axis_size("src")
    pairs = tile_index[0, 0]
    live = tile_count[0, 0]
    feats = edge_feature[0, 0]
    masks = edge_mask[0, 0]
    alive = (jnp.arange(slots, dtype=jnp.int32) < live).astype(f32)

    def gates_of(feat, row0, col0):
        src_rows = lax.dynamic_slice(gate_all, (col0, zero), (block, head_count))
        dst_rows = lax.dynamic_slice(target_all, (row0, zero), (block, head_count))
        return jax.nn.sigmoid(
            edge_scale[:, None, None] * feat.astype(f32)
            + src_rows.astype(f32).T[:, None, :]
            + dst_rows.astype(f32).T[:, :, None]
        )

    def values_of(col0):
        return lax.dynamic_slice(value_all, (col0, zero), (block, width)).reshape(
            block, head_count, size_head
        )

    def forward_tile(carry, item):
        numerator_total, denominator_total = carry
        pair, feat, mask_tile, flag = item
        row0 = pair[0] * block
        col0 = pair[1] * block
        sigma = gates_of(feat, row0, col0)
        gate = sigma * (mask_tile.astype(f32) * flag)[None]
        gate_low = gate.astype(low)
        tile_num = jnp.einsum(
            "kij,jke->ike", gate_low, values_of(col0), preferred_element_type=f32
        ).reshape(block, width)
        tile_den = jnp.sum(gate, axis=2).T
        numerator_total = lax.dynamic_update_slice(
            numerator_total,
            lax.dynamic_slice(numerator_total, (row0, zero), (block, width)) + tile_num,
            (row0, zero),
        )
        denominator_total = lax.dynamic_update_slice(
            denominator_total,
            lax.dynamic_slice(denominator_total, (row0, zero), (block, head_count)) + tile_den,
            (row0, zero),
        )
        return ((numerator_total, denominator_total), sigma)

    start = (jnp.zeros((dest_rows, width), f32), jnp.zeros((dest_rows, head_count), f32))
    (num_part, den_part), saved_gates = lax.scan(forward_tile, start, (pairs, feats, masks, alive))
    num_sum, den_sum = lax.psum((num_part, den_part), "src")
    first = lax.axis_index("src") * owned
    self_numerator = lax.dynamic_slice_in_dim(num_sum, first, owned, 0)
    self_denominator = lax.dynamic_slice_in_dim(den_sum, first, owned, 0)
    updated_node_features, denominator_floor, normalized_input, inverse_scale, normed_output = (
        node_update_forward(
            node_hidden_state,
            self_numerator,
            self_denominator,
            self_projection_weight,
            layer_norm_gain,
            head_count,
        )
    )
    preactivation_gradient, numerator_gradient, denominator_gradient = node_update_backward(
        cotangent,
        normed_output,
        normalized_input,
        inverse_scale,
        layer_norm_gain,
        self_numerator,
        denominator_floor,
        head_count,
    )
    num_rows_all, den_rows_all = (
        lax.all_gather(numerator_gradient, "src", axis=0, tiled=True),
        lax.all_gather(denominator_gradient, "src", axis=0, tiled=True),
    )

    def backward_tile(carry, item):
        grad_value, grad_gate, grad_target = carry
        pair, feat, mask_tile, flag, stored = item
        row0 = pair[0] * block
        col0 = pair[1] * block
        weight = mask_tile.astype(f32) * flag
        gate_low = (stored * weight[None]).astype(low)
        num_rows = lax.dynamic_slice(num_rows_all, (row0, zero), (block, width)).reshape(
            block, head_count, size_head
        )
        den_rows = lax.dynamic_slice(den_rows_all, (row0, zero), (block, head_count)).astype(f32)
        grad_sig = (
            jnp.einsum("ike,jke->kij", num_rows, values_of(col0), preferred_element_type=f32)
            + den_rows.T[:, :, None]
        )
        tile_value = jnp.einsum(
            "kij,ike->jke", gate_low, num_rows, preferred_element_type=f32
        ).reshape(block, width)
        grad_logit = grad_sig * weight[None] * stored * (1.0 - stored)
        grad_tile = (grad_logit * edge_scale[:, None, None]).astype(low)
        tile_gate = jnp.sum(grad_logit, axis=1).T
        tile_target = jnp.sum(grad_logit, axis=2).T
        grad_value = lax.dynamic_update_slice(
            grad_value,
            lax.dynamic_slice(grad_value, (col0, zero), (block, width)) + tile_value,
            (col0, zero),
        )
        grad_gate = lax.dynamic_update_slice(
            grad_gate,
            lax.dynamic_slice(grad_gate, (col0, zero), (block, head_count)) + tile_gate,
            (col0, zero),
        )
        grad_target = lax.dynamic_update_slice(
            grad_target,
            lax.dynamic_slice(grad_target, (row0, zero), (block, head_count)) + tile_target,
            (row0, zero),
        )
        return ((grad_value, grad_gate, grad_target), grad_tile)

    start = (
        jnp.zeros((group_rows, width), f32),
        jnp.zeros((group_rows, head_count), f32),
        jnp.zeros((dest_rows, head_count), f32),
    )
    (value_part, gate_part, target_part), grad_tiles = lax.scan(
        backward_tile, start, (pairs, feats, masks, alive, saved_gates)
    )
    target_sum = lax.psum(target_part, "src")
    target_own = lax.dynamic_slice_in_dim(target_sum, lax.axis_index("src") * owned, owned, 0)
    value_sum, gate_sum = lax.psum((value_part, gate_part), "dst")
    first = lax.axis_index("dst") * owned
    value_own = lax.dynamic_slice_in_dim(value_sum, first, owned, 0)
    gate_own = lax.dynamic_slice_in_dim(gate_sum, first, owned, 0)
    node_grad = (
        cotangent.astype(f32)
        + jnp.dot(
            preactivation_gradient.astype(low), self_projection_weight.T, preferred_element_type=f32
        )
        + jnp.dot(value_own.astype(low), weight_value.T, preferred_element_type=f32)
        + jnp.dot(gate_own.astype(low), weight_edge.T, preferred_element_type=f32)
        + jnp.dot(target_own.astype(low), weight_target.T, preferred_element_type=f32)
    )
    edge_grad = grad_tiles.reshape(1, 1, slots, head_count, block, block)
    return (updated_node_features, node_grad, edge_grad)


def solution(mesh):
    placed = (
        P(("dst", "src"), None),
        P(),
        P(),
        P(),
        P(),
        P(),
        P(),
        P("dst", "src", None, None),
        P("dst", "src"),
        P("dst", "src", None, None, None, None),
        P("dst", "src", None, None, None),
        P(("dst", "src"), None),
    )
    return jax.shard_map(
        body,
        mesh=mesh,
        in_specs=placed,
        out_specs=(
            P(("dst", "src"), None),
            P(("dst", "src"), None),
            P("dst", "src", None, None, None, None),
        ),
        check_vma=False,
    )
```

profile of v0, /device:TPU:1, one launch (start us, length us, event | category | flops | bytes accessed | tf_op | source)
XLA Modules:
  0.0 725.0 jit_solution(2793361250911359997)
XLA Ops:
  7.2 1.7 convolution_convert_fusion
  9.8 56.7 %all-gather = bf16[64,32,8]{1,2,0:T(8,128)(2,1)S(1)} all-gather(bf16[1,32,8]{1,2,0:T(8,128)(2,1)S(1)} %fusion.32), channel_id=1, replica_groups=mesh['dst'=64,'src'=12] {'dst'}, dimensions={0}, use_global_device_ids=true | all-gather | bytes 33280 | tf_op jit(solution)/shard_map/all_gather | solution.py:94
  67.6 22.6 %all-gather.1 = bf16[12,32,8]{1,2,0:T(8,128)(2,1)S(1)} all-gather(bf16[1,32,8]{1,2,0:T(8,128)(2,1)S(1)} %fusion.33), channel_id=1, replica_groups=mesh['dst'=64,'src'=12] {'src'}, dimensions={0}, use_global_device_ids=true | all-gather | bytes 6656 | tf_op jit(solution)/shard_map/all_gather | solution.py:96
  91.0 16.6 %all-gather.5.cloned.1.call-done = bf16[2048,256]{1,0:T(8,128)(2,1)} async-done(((bf16[32,256]{1,0:T(8,128)(2,1)}), bf16[2048,256]{1,0:T(8,128)(2,1)}) %all-gather.5.cloned.1.call-update) | async-done | bytes 1048592 | tf_op jit(solution)/shard_map/all_gather | solution.py:93
  107.6 1.5 copy.31
  109.2 72.0 %while.30 = (s32[]{:T(128)}, f32[384,256]{1,0:T(8,128)S(1)}, f32[384,8]{0,1:T(8,128)S(1)}, f32[8,8,128,128]{3,2,1,0:T(8,128)}, s32[8,2]{0,1:T(2,128)S(1)}, /*ind...) while((s32[]{:T(128)}, f32[384,256]{1,0:T(8,128)S(1)}, ...), condition=%wide.region_2.3_spmd, body=%wide.region_0.2_spmd.sunk | while | flops 11733002 | bytes 3396029 | solution.py:144
  111.9 1.5 multiply_bitcast_fusion.4
  113.4 1.3 fusion.82
  114.8 1.4 fusion.83
  116.2 2.0 fusion.85
  120.9 1.5 multiply_bitcast_fusion.4
  122.4 1.3 fusion.82
  123.8 1.4 fusion.83
  125.2 2.0 fusion.85
  129.9 1.5 multiply_bitcast_fusion.4
  131.4 1.3 fusion.82
  132.8 1.4 fusion.83
  134.2 2.0 fusion.85
  138.9 1.5 multiply_bitcast_fusion.4
  140.4 1.3 fusion.82
  141.8 1.4 fusion.83
  143.2 2.0 fusion.85
  147.9 1.5 multiply_bitcast_fusion.4
  149.4 1.3 fusion.82
  150.9 1.4 fusion.83
  152.2 2.0 fusion.85
  156.9 1.5 multiply_bitcast_fusion.4
  158.4 1.3 fusion.82
  159.8 1.4 fusion.83
  161.2 2.0 fusion.85
  165.9 1.5 multiply_bitcast_fusion.4
  167.4 1.3 fusion.82
  168.8 1.4 fusion.83
  170.2 2.0 fusion.85
  174.9 1.5 multiply_bitcast_fusion.4
  176.4 1.3 fusion.82
  177.8 1.4 fusion.83
  179.2 2.0 fusion.85
  182.2 37.4 %psum.36 = f32[384,8]{1,0:T(8,128)S(1)} all-reduce(f32[384,8]{1,0:T(8,128)S(1)} %copy.33), channel_id=1, replica_groups=mesh['dst'=64,'src'=12] {'src'}, use_global_device_ids=true, to_apply=%region_4.5 | all-reduce | flops 3072 | bytes 24576 | tf_op jit(solution)/shard_map/psum | solution.py:145
  219.8 65.0 %all-reduce.4.cloned.1.call-done = f32[384,256]{1,0:T(8,128)} async-done(((f32[384,256]{1,0:T(8,128)}), f32[384,256]{1,0:T(8,128)}) %all-reduce.4.cloned.1.call-update) | async-done | bytes 393232 | tf_op jit(solution)/shard_map/psum | solution.py:145
  288.0 18.3 %all_gather.18 = bf16[384,256]{1,0:T(8,128)(2,1)} all-gather(bf16[32,256]{1,0:T(8,128)(2,1)S(1)} %divide_convert_fusion), channel_id=1, replica_groups=mesh['dst'=64,'src'=12] {'src'}, dimensions={0}, use_global_device_ids=true | all-gather | bytes 212992 | tf_op jit(solution)/shard_map/all_gather | solution.py:170
  306.6 15.1 %all-gather.2 = bf16[12,32,8]{1,2,0:T(8,128)(2,1)S(1)} all-gather(bf16[1,32,8]{1,2,0:T(8,128)(2,1)S(1)} %copy.34), channel_id=1, replica_groups=mesh['dst'=64,'src'=12] {'src'}, dimensions={0}, use_global_device_ids=true | all-gather | bytes 6656 | tf_op jit(solution)/shard_map/all_gather | solution.py:171
  322.0 69.2 %while.31 = (s32[]{:T(128)}, f32[2048,256]{0,1:T(8,128)S(1)}, f32[2048,8]{0,1:T(8,128)S(1)}, f32[384,8]{0,1:T(8,128)S(1)}, bf16[8,8,128,128]{3,2,1,0:T(8,128)(2,...) while((s32[]{:T(128)}, f32[2048,256]{0,1:T(8,128)S(1)}, ...), condition=%wide.region_13.14_spmd, body=%wide.region_10.13_spmd.sunk | while | flops 18285576 | bytes 3778949 | solution.py:218
  325.6 1.4 multiply_bitcast_fusion.5
  327.0 1.2 fusion.91
  328.3 1.5 fusion.92
  334.2 1.4 multiply_bitcast_fusion.5
  335.6 1.2 fusion.91
  337.0 1.5 fusion.92
  342.9 1.4 multiply_bitcast_fusion.5
  344.3 1.2 fusion.91
  345.6 1.5 fusion.92
  351.5 1.4 multiply_bitcast_fusion.5
  354.3 1.5 fusion.92
  360.2 1.4 multiply_bitcast_fusion.5
  362.9 1.5 fusion.92
  368.8 1.4 multiply_bitcast_fusion.5
  371.6 1.5 fusion.92
  377.5 1.4 multiply_bitcast_fusion.5
  380.2 1.5 fusion.92
  386.1 1.4 multiply_bitcast_fusion.5
  388.9 1.5 fusion.92
  391.2 31.7 %psum.39 = bf16[384,8]{0,1:T(8,128)(2,1)S(1)} all-reduce(f32[384,8]{0,1:T(8,128)S(1)} %get-tuple-element.142), channel_id=1, replica_groups=mesh['dst'=64,'src'=12] {'src'}, use_global_device_ids=true, to_apply=%region_16.17 | all-reduce | flops 3072 | bytes 18432 | tf_op jit(solution)/shard_map/psum | solution.py:221
  423.0 293.0 %all-reduce.5 = (bf16[2048,256]{0,1:T(8,128)(2,1)}, bf16[2048,8]{0,1:T(8,128)(2,1)S(1)}) all-reduce(f32[2048,256]{0,1:T(8,128)S(1)} %get-tuple-element.140, f32[2048,8]{0,1:T(8,128)S(1)} %get-tuple-element.141), channel_id=1, replica_groups=mesh['dst'=64,'src'=12] {'dst'}, use_global_device_ids=true, to_apply=%region_14.15 | all-reduce | flops 540672 | bytes 3244032 | tf_op jit(solution)/shard_map/psum | solution.py:223
  (233 shorter events, 52.0 us)
Async XLA Ops:
  7.2 277.7 %copy-start = (bf16[256,256]{1,0:T(8,128)(2,1)S(1)}, bf16[256,256]{1,0:T(8,128)(2,1)}, u32[]{:S(2)}) copy-start(bf16[256,256]{1,0:T(8,128)(2,1)} %param.17) | copy-start | bytes 393220
  7.2 102.0 %copy-start.5 = (s32[1,1,8,2]{2,3,1,0:T(2,128)S(1)}, s32[1,1,8,2]{2,3,1,0:T(2,128)}, u32[]{:S(2)}) copy-start(s32[1,1,8,2]{2,3,1,0:T(2,128)} %param.23) | copy-start | bytes 196
  7.2 102.0 %copy-start.4 = (f32[8]{0:T(128)S(1)}, f32[8]{0:T(128)}, u32[]{:S(2)}) copy-start(f32[8]{0:T(128)} %param.22) | copy-start | bytes 100
  7.2 100.4 %all-gather.5.cloned.1.call-start = ((), (), s32[]{:S(2)}) async-start(), calls=%async_computation | async-start | bytes 1064960 | tf_op jit(solution)/shard_map/all_gather | solution.py:93
  9.0 275.9 %all-reduce.4.cloned.1.call-start = ((), (), s32[]{:S(2)}) async-start(), calls=%async_computation.1 | async-start | bytes 786432 | tf_op jit(solution)/shard_map/psum | solution.py:145
  109.2 175.7 %copy-start.3 = (bf16[32,256]{1,0:T(8,128)(2,1)S(1)}, bf16[32,256]{1,0:T(8,128)(2,1)}, u32[]{:S(2)}) copy-start(bf16[32,256]{1,0:T(8,128)(2,1)} %param.16) | copy-start | bytes 49156
  109.2 176.9 %copy-start.6 = (bf16[32,256]{1,0:T(8,128)(2,1)S(1)}, bf16[32,256]{1,0:T(8,128)(2,1)}, u32[]{:S(2)}) copy-start(bf16[32,256]{1,0:T(8,128)(2,1)} %param.27) | copy-start | bytes 49156
  109.2 176.9 %copy-start.9 = (f32[256]{0:T(256)S(1)}, f32[256]{0:T(256)}, u32[]{:S(2)}) copy-start(f32[256]{0:T(256)} %param.21) | copy-start | bytes 3076
  181.2 0.7 copy-start.1
  391.2 324.7 %copy-start.2 = (bf16[256,256]{1,0:T(8,128)(2,1)S(1)}, bf16[256,256]{1,0:T(8,128)(2,1)}, u32[]{:S(2)}) copy-start(bf16[256,256]{1,0:T(8,128)(2,1)} %param.18) | copy-start | bytes 393220
  391.2 325.8 %copy-start.7 = (bf16[256,8]{0,1:T(8,128)(2,1)S(1)}, bf16[256,8]{0,1:T(8,128)(2,1)}, u32[]{:S(2)}) copy-start(bf16[256,8]{0,1:T(8,128)(2,1)} %param.19) | copy-start | bytes 12292
  391.2 326.0 %copy-start.8 = (bf16[256,8]{0,1:T(8,128)(2,1)S(1)}, bf16[256,8]{0,1:T(8,128)(2,1)}, u32[]{:S(2)}) copy-start(bf16[256,8]{0,1:T(8,128)(2,1)} %param.20) | copy-start | bytes 12292
Sparse Core Ops, SparseCore 0:
  12.6 95.0 all-gather.4
  182.1 102.6 all-reduce.3
where the time goes:
time: 730 us; the launch traced here: 725 us
  blocking collectives  475 us (65%)
  waiting for transfers between devices  81.7 us (11%)
  other arithmetic  59.5 us (8%)
  matrix products  39.4 us (5%)
  local copies, waits for them, and re-layouts  32.9 us (5%)
  loops' own time  21.7 us (3%)
  between operations  15 us (2%)
    psum x1, blocking collectives, body(): value_sum, gate_sum = lax.psum((value_part, gate_part), 'dst')  293 us
    psum x1, waiting for transfers between devices, body(): num_sum, den_sum = lax.psum((num_part, den_part), 'src')  65 us
    all_gather x1, blocking collectives, body(): lax.all_gather(source_gate, 'dst', axis=0, tiled=True)  56.7 us
    psum x1, blocking collectives, body(): num_sum, den_sum = lax.psum((num_part, den_part), 'src')  37.4 us
    psum x1, blocking collectives, body(): target_sum = lax.psum(target_part, 'src')  31.7 us
    all_gather x1, blocking collectives, body(): target_all = lax.all_gather(target_gate, 'src', axis=0, tiled=True)  22.6 us
    all_gather x1, blocking collectives, body(): lax.all_gather(numerator_gradient, 'src', axis=0, tiled=True)  18.3 us
    all_gather x1, waiting for transfers between devices, body(): lax.all_gather(value, 'dst', axis=0, tiled=True)  16.6 us
  transfers between devices with their start and end apart: 2, of which 2 were waited for; matrix products, arithmetic and copies ran while one was open for 0% of the time, Pallas kernels for 0%

commit v1 on v0

v1 whole, which is shorter than its diff:
```python
import functools

import jax
import jax.numpy as jnp
from jax import lax
from jax.experimental import pallas as pl
from jax.experimental.pallas import tpu as pltpu
from jax.sharding import PartitionSpec as P

F32 = jnp.float32
LOW = jnp.bfloat16
D = 256
HEADS = 8
HALF = 4
TB = 128
SH = D // HEADS
MESH = pl.DeviceIdType.MESH
NT = (((1,), (1,)), ((), ()))


def mm(a, b):
    return jnp.dot(a, b, preferred_element_type=F32)


def mm_nt(a, b):
    return lax.dot_general(a, b, NT, preferred_element_type=F32)


def mm_exact(a, b):
    return jnp.dot(a, b, preferred_element_type=F32, precision=lax.Precision.HIGHEST)


def iota(shape, dim):
    return lax.broadcasted_iota(jnp.int32, shape, dim)


def kernel(
    shape,
    scale_ref, pair_ref, count_ref,
    h_ref, cot_ref, wet_ref, wtt_ref, gain_ref,
    wself_hbm, wvalue_hbm, feat_hbm, mask_hbm,
    out_ref, grad_ref, edge_hbm,
    wself, wvalue, feat, mask, hbuf, tbuf, gate32, gate16, vmask, nt, onehot, spread,
    send0, send1, recv0, recv1, dbuf, dnt, egbuf, pt, wproj, lut, dtbuf,
    dpart, rcore, s1, rx, s2, ry, dtsend, dtrecv,
    lsem, esem,
    ysend, yrecv, xsend, xrecv, csend, crecv, tsend, trecv,
    z0send, z0recv, z1send, z1recv, dsend, drecv,
    bcsend, bcrecv, bxsend, bxrecv, bysend, byrecv, gsend, grecv,
):
    nx, ny, nz, nd, slots = shape
    rb = nz * nd // TB
    cb = nx * ny * 2 * nd // TB
    cbx = cb // nx
    dst = lax.axis_index("dst")
    z = lax.axis_index("src")
    x = dst // (ny * 2)
    y = lax.rem(dst // 2, ny)
    c = lax.rem(dst, 2)

    def at_y(v):
        return {"dst": (x * ny + v) * 2 + c, "src": z}

    def at_x(v):
        return {"dst": (v * ny + y) * 2 + c, "src": z}

    def at_z(v):
        return {"dst": dst, "src": v}

    sibling = {"dst": (x * ny + y) * 2 + 1 - c, "src": z}

    def remote(src, dst_ref, ssem, rsem, device):
        return pltpu.make_async_remote_copy(
            src_ref=src, dst_ref=dst_ref, send_sem=ssem, recv_sem=rsem,
            device_id=device, device_id_type=MESH,
        )

    loads = [
        pltpu.make_async_copy(wvalue_hbm, wvalue, lsem.at[0]),
        pltpu.make_async_copy(wself_hbm, wself, lsem.at[1]),
        pltpu.make_async_copy(mask_hbm.at[0, 0], mask, lsem.at[2]),
        pltpu.make_async_copy(feat_hbm.at[0, 0], feat, lsem.at[3]),
    ]
    for load in loads:
        load.start()

    barrier = pltpu.get_barrier_semaphore()
    for d in range(1, ny):
        pl.semaphore_signal(barrier, inc=1, device_id=at_y(lax.rem(y + d, ny)), device_id_type=MESH)
    for d in range(1, nx):
        pl.semaphore_signal(barrier, inc=1, device_id=at_x(lax.rem(x + d, nx)), device_id_type=MESH)
    for d in range(1, nz):
        pl.semaphore_signal(barrier, inc=1, device_id=at_z(lax.rem(z + d, nz)), device_id_type=MESH)
    pl.semaphore_signal(barrier, inc=1, device_id=sibling, device_id_type=MESH)

    h = h_ref[...]
    hbuf[x, y, c] = h
    wtt = jnp.concatenate([wtt_ref[...].astype(F32), jnp.zeros((TB - HEADS, D), F32)], axis=0).astype(LOW)
    wet32 = jnp.concatenate([wet_ref[...].astype(F32), jnp.zeros((TB - HEADS, D), F32)], axis=0)
    wet = wet32[:16].astype(LOW)
    tbuf[z] = mm_nt(h, wtt).astype(LOW)

    pl.semaphore_wait(barrier, ny + nx + nz - 2)

    for d in range(1, ny):
        remote(h_ref, hbuf.at[x, y, c], ysend.at[d], yrecv.at[d], at_y(lax.rem(y + d, ny))).start()
    for d in range(1, nz):
        remote(tbuf.at[z], tbuf.at[z], tsend.at[d], trecv.at[d], at_z(lax.rem(z + d, nz))).start()

    count = count_ref[0, 0]
    rows = [jnp.clip(pair_ref[0, 0, t, 0], 0, rb - 1) for t in range(slots)]
    cols = [jnp.clip(pair_ref[0, 0, t, 1], 0, cb - 1) for t in range(slots)]
    live = [jnp.where(count > t, 1.0, 0.0).astype(F32) for t in range(slots)]

    def fill_lut(q, carry):
        for r in range(rb):
            found = jnp.int32(slots)
            for t in range(slots):
                hit = (rows[t] == r) & (cols[t] == q) & (count > t)
                found = jnp.where(hit, jnp.int32(t), found)
            lut[q, r] = found
        return carry

    lax.fori_loop(0, cb, fill_lut, 0)
    lane = iota((TB, TB), 1)
    for half in range(2):
        for k in range(HALF):
            onehot[half, k * TB:(k + 1) * TB, :] = jnp.where(lane == half * HALF + k, 1.0, 0.0).astype(LOW)
            spread[half, :, k * TB:(k + 1) * TB] = jnp.where(
                iota((TB, TB), 0) == half * HALF + k, 0.5, 0.0
            ).astype(LOW)
    pt[slots] = jnp.zeros((TB, D), F32)
    loads[0].wait()
    wproj[:, 0:D] = wvalue[...]
    wproj[:, D:D + TB] = wet32.T.astype(LOW)
    loads[1].wait()
    self_pre = mm(h, wself[...])

    for d in range(1, ny):
        v = lax.rem(y + ny - d, ny)
        remote(hbuf.at[x, v, c], hbuf.at[x, v, c], ysend.at[d], yrecv.at[d], at_y(v)).wait_recv()
    for d in range(1, nx):
        remote(hbuf.at[x, :, c], hbuf.at[x, :, c], xsend.at[d], xrecv.at[d], at_x(lax.rem(x + d, nx))).start()
    remote(hbuf.at[x, :, c], hbuf.at[x, :, c], csend.at[0], crecv.at[0], sibling).start()
    for d in range(1, nx):
        v = lax.rem(x + nx - d, nx)
        remote(hbuf.at[v, :, c], hbuf.at[v, :, c], xsend.at[d], xrecv.at[d], at_x(v)).wait_recv()
        remote(hbuf.at[v, :, c], hbuf.at[v, :, c], csend.at[d], crecv.at[d], sibling).start()
    for d in range(1, nz):
        v = lax.rem(z + nz - d, nz)
        remote(tbuf.at[v], tbuf.at[v], tsend.at[d], trecv.at[d], at_z(v)).wait_recv()
    loads[2].wait()
    loads[3].wait()
    for d in range(nx):
        v = lax.rem(x + nx - d, nx)
        remote(hbuf.at[v, :, 1 - c], hbuf.at[v, :, 1 - c], csend.at[d], crecv.at[d], sibling).wait_recv()

    def h_tile(col):
        per = cbx
        xi = col // per
        q = lax.rem(col, per)
        step = ny // per
        return hbuf[xi, pl.ds(q * step, step)].reshape(TB, D)

    def tile_scalars(t):
        row = jnp.clip(pair_ref[0, 0, t, 0], 0, rb - 1)
        col = jnp.clip(pair_ref[0, 0, t, 1], 0, cb - 1)
        return row, col, jnp.where(count > t, 1.0, 0.0).astype(F32)

    lane_d = iota((TB, D), 1) // SH

    def t_rows(row):
        per = TB // nd
        return tbuf[pl.ds(row * per, per)].reshape(TB, TB)

    def forward(half):
        def step(t, carry):
            row, col, flag = tile_scalars(t)
            ht = h_tile(col)
            val = mm(ht, wvalue[:, half * TB:(half + 1) * TB])
            src = mm_nt(wet, ht).astype(LOW).astype(F32) * 0.5
            outer = mm(t_rows(row), spread[half])
            weight = mask[t].astype(F32) * flag
            gates = []
            for k in range(HALF):
                kk = half * HALF + k
                vmask[t, half, k * TB:(k + 1) * TB, :] = jnp.where(
                    lane // SH == k, val, 0.0
                ).astype(LOW)
                arg = feat[t, kk].astype(F32) * (scale_ref[kk] * 0.5) + (
                    outer[:, k * TB:(k + 1) * TB] + src[kk:kk + 1, :]
                )
                gate = (0.5 * jnp.tanh(arg) + 0.5) * weight
                gate32[t, kk] = gate
                low = gate.astype(LOW)
                gate16[t, kk] = low
                gates.append(low)
            rhs = jnp.concatenate([vmask[t, half], onehot[half]], axis=1)
            nt[half, t] = mm(jnp.concatenate(gates, axis=1), rhs)
            return carry

        lax.fori_loop(0, slots, step, 0)

    per = TB // nd

    def row_sums(lanes, parts):
        for r in range(rb):
            sel = [jnp.where(rows[t] == r, 1.0, 0.0).astype(F32) for t in range(slots)]
            total = jnp.zeros((TB, lanes), F32)
            for half, start in parts:
                for t in range(slots):
                    total += nt[half, t, :, start:start + lanes] * sel[t]
            yield r, total

    forward(0)
    for r, total in row_sums(TB, [(0, 0)]):
        send0[r * per:(r + 1) * per] = total.astype(LOW).reshape(per, nd, TB)
    for d in range(1, nz):
        v = lax.rem(z + d, nz)
        remote(send0.at[v], recv0.at[d], z0send.at[d], z0recv.at[d], at_z(v)).start()
    forward(1)
    for r, total in row_sums(TB, [(1, 0)]):
        send1[r * per:(r + 1) * per, :, 0:TB] = total.astype(LOW).reshape(per, nd, TB)
    for r, total in row_sums(TB, [(0, TB), (1, TB)]):
        send1[r * per:(r + 1) * per, :, TB:D] = total.astype(LOW).reshape(per, nd, TB)
    for d in range(1, nz):
        v = lax.rem(z + d, nz)
        remote(send1.at[v], recv1.at[d], z1send.at[d], z1recv.at[d], at_z(v)).start()

    def slope(t, carry):
        for k in range(HEADS):
            g = gate32[t, k]
            gate32[t, k] = g - g * g
        return carry

    lax.fori_loop(0, slots, slope, 0)

    num0 = send0[z].astype(F32)
    both = send1[z].astype(F32)
    for d in range(1, nz):
        remote(recv0.at[d], recv0.at[d], z0send.at[d], z0recv.at[d], at_z(z)).wait_recv()
        num0 += recv0[d].astype(F32)
    for d in range(1, nz):
        remote(recv1.at[d], recv1.at[d], z1send.at[d], z1recv.at[d], at_z(z)).wait_recv()
        both += recv1[d].astype(F32)

    num = jnp.concatenate([num0, both[:, 0:TB]], axis=1)
    floor = both[:, TB:D] + 1.0
    expand = jnp.where(iota((TB, D), 0) == lane_d, 1.0, 0.0).astype(F32)
    floor_d = mm_exact(floor, expand)
    pre = self_pre + num / floor_d
    centred = pre - jnp.mean(pre, axis=-1, keepdims=True)
    inv = lax.rsqrt(jnp.mean(centred * centred, axis=-1, keepdims=True) + 1e-05)
    xhat = centred * inv
    gain = gain_ref[...]
    yv = xhat * gain
    sg = jax.nn.sigmoid(yv)
    cot = cot_ref[...].astype(F32)
    out_ref[...] = (h.astype(F32) + yv * sg).astype(LOW)
    dx = cot * sg * (1.0 + yv * (1.0 - sg)) * gain
    dpre = inv * (
        dx - jnp.mean(dx, axis=-1, keepdims=True) - xhat * jnp.mean(dx * xhat, axis=-1, keepdims=True)
    )
    collect = jnp.where(iota((D, TB), 0) // SH == iota((D, TB), 1), 1.0, 0.0).astype(F32)
    dden = -mm_exact(dpre * num, collect) / (floor * floor)
    dbuf[z] = jnp.concatenate([dpre / floor_d, dden], axis=1).astype(LOW)
    for d in range(1, nz):
        remote(dbuf.at[z], dbuf.at[z], dsend.at[d], drecv.at[d], at_z(lax.rem(z + d, nz))).start()
    own_grad = cot + mm_nt(dpre.astype(LOW), wself[...])
    for d in range(1, nz):
        v = lax.rem(z + nz - d, nz)
        remote(dbuf.at[v], dbuf.at[v], dsend.at[d], drecv.at[d], at_z(v)).wait_recv()

    for r in range(rb):
        block = dbuf[r * per:(r + 1) * per, :, 0:D].reshape(TB, D).astype(F32)
        dnt[r] = block.T.astype(LOW)

    def backward(t, carry):
        row, col, flag = tile_scalars(t)
        dn = dbuf[pl.ds(row * per, per)].reshape(TB, D + TB)
        dnr = dnt[row]
        grads = []
        dt = jnp.zeros((TB, TB), F32)
        sums = []
        for half in range(2):
            lhs = jnp.concatenate([dn[:, half * TB:(half + 1) * TB], dn[:, D:D + TB]], axis=1)
            rhs = jnp.concatenate([vmask[t, half], onehot[half]], axis=1)
            dsig = mm_nt(lhs, rhs)
            lows = []
            for k in range(HALF):
                kk = half * HALF + k
                dl = dsig[:, k * TB:(k + 1) * TB] * gate32[t, kk]
                egbuf[t, kk] = (dl * scale_ref[kk]).astype(LOW)
                sums.append(jnp.sum(dl, axis=0, keepdims=True))
                lows.append(dl.astype(LOW))
                grads.append(mm(dnr[kk * SH:(kk + 1) * SH, :], gate16[t, kk]))
            dt += mm(jnp.concatenate(lows, axis=1), onehot[half])
        dtbuf[t] = dt
        pltpu.make_async_copy(egbuf.at[t], edge_hbm.at[0, 0, t], esem.at[t]).start()
        stack = jnp.concatenate(grads + sums + [jnp.zeros((TB - HEADS, TB), F32)], axis=0).astype(LOW)
        pt[t] = mm(wproj[...], stack).T
        return carry

    lax.fori_loop(0, slots, backward, 0)

    for r in range(rb):
        total = jnp.zeros((TB, TB), F32)
        for t in range(slots):
            total += dtbuf[t] * jnp.where(rows[t] == r, 1.0, 0.0).astype(F32)
        dtsend[r * per:(r + 1) * per] = total.astype(LOW).reshape(per, nd, TB)

    def quarter(xi):
        def one(q, carry):
            block = xi * cbx + q
            total = pt[lut[block, 0]]
            for r in range(1, rb):
                total += pt[lut[block, r]]
            step = ny // cbx
            dpart[xi, pl.ds(q * step, step)] = total.astype(LOW).reshape(step, 2, nd, D)
            return carry

        lax.fori_loop(0, cbx, one, 0)

    for d in range(nx):
        v = lax.rem(x + 1 + d, nx)
        quarter(v)
        remote(dpart.at[v, :, 1 - c], rcore.at[v], bcsend.at[d], bcrecv.at[d], sibling).start()
        if d == 0:
            for e in range(1, nz):
                w = lax.rem(z + e, nz)
                remote(dtsend.at[w], dtrecv.at[e], gsend.at[e], grecv.at[e], at_z(w)).start()
    for d in range(nx):
        v = lax.rem(x + 1 + d, nx)
        remote(rcore.at[v], rcore.at[v], bcsend.at[d], bcrecv.at[d], sibling).wait_recv()
        s1[v] = (dpart[v, :, c].astype(F32) + rcore[v].astype(F32)).astype(LOW)
        if d < nx - 1:
            remote(s1.at[v], rx.at[d], bxsend.at[d], bxrecv.at[d], at_x(v)).start()
    total = s1[x].astype(F32)
    for d in range(nx - 1):
        remote(rx.at[d], rx.at[d], bxsend.at[d], bxrecv.at[d], at_x(x)).wait_recv()
        total += rx[d].astype(F32)
    s2[...] = total.astype(LOW)
    for d in range(1, ny):
        v = lax.rem(y + d, ny)
        remote(s2.at[v], ry.at[d], bysend.at[d], byrecv.at[d], at_y(v)).start()
    dt = dtsend[z].astype(F32)
    for d in range(1, nz):
        remote(dtrecv.at[d], dtrecv.at[d], gsend.at[d], grecv.at[d], at_z(z)).wait_recv()
        dt += dtrecv[d].astype(F32)
    own_grad = own_grad + mm(dt.astype(LOW), wtt)
    final = s2[y].astype(F32)
    for d in range(1, ny):
        remote(ry.at[d], ry.at[d], bysend.at[d], byrecv.at[d], at_y(y)).wait_recv()
        final += ry[d].astype(F32)
    grad_ref[...] = own_grad + final

    for d in range(1, ny):
        remote(h_ref, h_ref, ysend.at[d], yrecv.at[d], at_y(y)).wait_send()
        remote(s2.at[y], s2.at[y], bysend.at[d], byrecv.at[d], at_y(y)).wait_send()
    for d in range(1, nx):
        remote(hbuf.at[x, :, c], hbuf.at[x, :, c], xsend.at[d], xrecv.at[d], at_x(x)).wait_send()
        remote(s1.at[x], s1.at[x], bxsend.at[d - 1], bxrecv.at[d - 1], at_x(x)).wait_send()
    for d in range(nx):
        remote(hbuf.at[x, :, c], hbuf.at[x, :, c], csend.at[d], crecv.at[d], sibling).wait_send()
        remote(rcore.at[x], rcore.at[x], bcsend.at[d], bcrecv.at[d], sibling).wait_send()
    for d in range(1, nz):
        remote(tbuf.at[z], tbuf.at[z], tsend.at[d], trecv.at[d], at_z(z)).wait_send()
        remote(send0.at[z], send0.at[z], z0send.at[d], z0recv.at[d], at_z(z)).wait_send()
        remote(send1.at[z], send1.at[z], z1send.at[d], z1recv.at[d], at_z(z)).wait_send()
        remote(dbuf.at[z], dbuf.at[z], dsend.at[d], drecv.at[d], at_z(z)).wait_send()
        remote(dtsend.at[z], dtsend.at[z], gsend.at[d], grecv.at[d], at_z(z)).wait_send()
    for t in range(slots):
        pltpu.make_async_copy(egbuf.at[t], edge_hbm.at[0, 0, t], esem.at[t]).wait()


def body(
    nx, ny,
    node_hidden_state, self_projection_weight, weight_value, weight_edge, weight_target,
    layer_norm_gain, edge_scale, tile_index, tile_count, edge_feature, edge_mask, cotangent,
):
    nd = node_hidden_state.shape[0]
    nz = lax.axis_size("src")
    slots = edge_mask.shape[2]
    rb = nz * nd // TB
    cb = nx * ny * 2 * nd // TB
    vmem = pl.BlockSpec(memory_space=pltpu.VMEM)
    smem = pl.BlockSpec(memory_space=pltpu.SMEM)
    hbm = pl.BlockSpec(memory_space=pl.ANY)
    scratch = [
        pltpu.VMEM((D, D), LOW),
        pltpu.VMEM((D, D), LOW),
        pltpu.VMEM((slots, HEADS, TB, TB), LOW),
        pltpu.VMEM((slots, TB, TB), jnp.int32),
        pltpu.VMEM((nx, ny, 2, nd, D), LOW),
        pltpu.VMEM((nz, nd, TB), LOW),
        pltpu.VMEM((slots, HEADS, TB, TB), F32),
        pltpu.VMEM((slots, HEADS, TB, TB), LOW),
        pltpu.VMEM((slots, 2, HALF * TB, TB), LOW),
        pltpu.VMEM((2, slots, TB, D), F32),
        pltpu.VMEM((2, HALF * TB, TB), LOW),
        pltpu.VMEM((2, TB, HALF * TB), LOW),
        pltpu.VMEM((nz, nd, TB), LOW),
        pltpu.VMEM((nz, nd, D), LOW),
        pltpu.VMEM((nz, nd, TB), LOW),
        pltpu.VMEM((nz, nd, D), LOW),
        pltpu.VMEM((nz, nd, D + TB), LOW),
        pltpu.VMEM((rb, D, TB), LOW),
        pltpu.VMEM((slots, HEADS, TB, TB), LOW),
        pltpu.VMEM((slots + 1, TB, D), F32),
        pltpu.VMEM((D, D + TB), LOW),
        pltpu.SMEM((cb, rb), jnp.int32),
        pltpu.VMEM((slots, TB, TB), F32),
        pltpu.VMEM((nx, ny, 2, nd, D), LOW),
        pltpu.VMEM((nx, ny, nd, D), LOW),
        pltpu.VMEM((nx, ny, nd, D), LOW),
        pltpu.VMEM((nx, ny, nd, D), LOW),
        pltpu.VMEM((ny, nd, D), LOW),
        pltpu.VMEM((ny, nd, D), LOW),
        pltpu.VMEM((nz, nd, TB), LOW),
        pltpu.VMEM((nz, nd, TB), LOW),
        pltpu.SemaphoreType.DMA((4,)),
        pltpu.SemaphoreType.DMA((slots,)),
    ]
    for n in (ny, nx, nx, nz, nz, nz, nz, nx, nx, ny, nz):
        scratch += [pltpu.SemaphoreType.DMA((n,)), pltpu.SemaphoreType.DMA((n,))]
    return pl.pallas_call(
        functools.partial(kernel, (nx, ny, nz, nd, slots)),
        out_shape=(
            jax.ShapeDtypeStruct((nd, D), LOW),
            jax.ShapeDtypeStruct((nd, D), F32),
            jax.ShapeDtypeStruct((1, 1, slots, HEADS, TB, TB), LOW),
        ),
        in_specs=[smem, smem, smem, vmem, vmem, vmem, vmem, vmem, hbm, hbm, hbm, hbm],
        out_specs=(vmem, vmem, hbm),
        scratch_shapes=scratch,
        compiler_params=pltpu.CompilerParams(
            collective_id=0, has_side_effects=True, vmem_limit_bytes=48 * 1024 * 1024
        ),
        name="gated_conv",
    )(
        edge_scale, tile_index, tile_count,
        node_hidden_state, cotangent, weight_edge.T, weight_target.T, layer_norm_gain[None, :],
        self_projection_weight, weight_value, edge_feature, edge_mask,
    )


def build(mesh, nx, ny):
    placed = (
        P(("dst", "src"), None), P(), P(), P(), P(), P(), P(),
        P("dst", "src", None, None), P("dst", "src"),
        P("dst", "src", None, None, None, None), P("dst", "src", None, None, None),
        P(("dst", "src"), None),
    )
    return jax.shard_map(
        functools.partial(body, nx, ny),
        mesh=mesh,
        in_specs=placed,
        out_specs=(
            P(("dst", "src"), None),
            P(("dst", "src"), None),
            P("dst", "src", None, None, None, None),
        ),
        check_vma=False,
    )


def solution(mesh):
    return build(mesh, 4, 8)
```

time: 730 us -> 99.9 us (0.14)
  blocking collectives: 475 us -> 0 us
  Pallas kernels: 0 us -> 86.3 us
  waiting for transfers between devices: 81.7 us -> 0 us
  other arithmetic: 59.5 us -> 0 us
  matrix products: 39.4 us -> 0 us
  loops' own time: 21.7 us -> 0 us
  local copies, waits for them, and re-layouts: 32.9 us -> 11.9 us
  between operations: 15 us -> 1.3 us
    psum x3 -> x0, blocking collectives: 362 us -> none  [the longest x1 293 us: body(): value_sum, gate_sum = lax.psum((value_part, gate_part), 'dst')]
    all_gather x4 -> x0, blocking collectives: 113 us -> none  [the longest x1 56.7 us: body(): lax.all_gather(source_gate, 'dst', axis=0, tiled=True)]
    pallas_call x0 -> x1, Pallas kernels: none -> 86.3 us  [body(): pl.pallas_call(functools.partial(kernel, (nx, ny, nz, nd, slots)), out_sh...]
    psum x1 -> x0, waiting for transfers between devices: 65 us -> none  [body(): num_sum, den_sum = lax.psum((num_part, den_part), 'src')]
    dot_general x32 -> x0, matrix products: 39.4 us -> none  [the longest x8 12.4 us: backward_tile(): jnp.einsum('ike,jke->kij', num_rows, values_of(col0), preferred_element_t...]
    mul x17 -> x0, other arithmetic: 24.2 us -> none  [the longest x8 11.9 us: forward_tile(): gate = sigma * (mask_tile.astype(f32) * flag)[None]]
    dynamic_update_slice x40 -> x0, other arithmetic: 22.9 us -> none  [the longest x8 15.9 us: body(): lax.scan(forward_tile, start, (pairs, feats, masks, alive))]
    another operation x2 -> x0, loops' own time: 21.7 us -> none  [the longest x1 11.1 us: body(): lax.scan(forward_tile, start, (pairs, feats, masks, alive))]
  transfers between devices with their start and end apart: 2 -> 0, of which waited for: 2 -> 0; matrix products, arithmetic and copies ran while one was open for 0% -> 0% of each run, Pallas kernels for 0% -> 0%
where the time goes in v1:
time: 99.9 us; the launch traced here: 99.5 us
  Pallas kernels  86.3 us (86%)
  local copies, waits for them, and re-layouts  11.9 us (12%)
  between operations  1.3 us (1%)
    pallas_call x1, Pallas kernels, body(): pl.pallas_call(functools.partial(kernel, (nx, ny, nz, nd, slots)), out_sh...  86.3 us
    unnamed x24, local copies, waits for them, and re-layouts  11.9 us

profile of v1, /device:TPU:1, one launch (start us, length us, event | category | flops | bytes accessed | tf_op | source)
XLA Modules:
  0.0 99.5 jit_solution(14952133285310085358)
XLA Ops:
  1.3 0.8 copy.15.pair_ref
  2.0 0.0 copy-start
  2.0 1.6 %copy-done = bf16[1,1,8,8,128,128]{5,4,3,2,1,0:T(8,128)(2,1)S(1)} copy-done((bf16[1,1,8,8,128,128]{5,4,3,2,1,0:T(8,128)(2,1)S(1)}, bf16[1,1,8,8,128,128]{5,4,3,2,1,0:T(8,128)(2,1)}, u32[]{:S(2)}) %copy-start) | copy-done | bytes 2097176
  3.6 0.0 copy-start.1
  3.6 1.0 %copy-done.1 = s32[1,1,8,128,128]{4,3,2,1,0:T(8,128)S(1)} copy-done((s32[1,1,8,128,128]{4,3,2,1,0:T(8,128)S(1)}, s32[1,1,8,128,128]{4,3,2,1,0:T(8,128)}, u32[]{:S(2)}) %copy-start.1) | copy-done | bytes 524312
  4.7 0.0 copy-start.2
  4.7 0.9 copy-done.2
  5.6 0.0 copy-start.3
  5.6 0.9 copy-done.3
  6.5 0.0 copy-start.4
  6.5 0.7 copy-done.4
  7.2 0.0 copy-start.5
  7.2 0.7 copy-done.5
  7.9 0.0 copy-start.6
  7.9 0.7 copy-done.6
  8.6 0.0 copy-start.7
  8.6 0.7 copy-done.7
  9.3 0.0 copy-start.8
  9.3 0.7 copy-done.8
  10.0 0.0 copy-start.9
  10.0 0.7 copy-done.9
  10.6 86.3 %gated_conv.1 = (bf16[32,256]{1,0:T(8,128)(2,1)S(1)}, f32[32,256]{1,0:T(8,128)S(1)}, bf16[1,1,8,8,128,128]{5,4,3,2,1,0:T(8,128)(2,1)S(1)}) custom-call(f32[8]{0:T(128)S(1)} %copy-done.9, s32[1,1,8,2]{3,2,1,0:T(8,128)S(1)} %copy.15.pair_ref, s32[1,1]{1,0:T(1,128)S(6)} %copy.19.count_ref, bf16[32,256]{1,0:T(8,128)(2,1)S(1)} %copy-done.4, ...), custom_call_target="tpu_custom_call" | custom-call | tf_op jit(solution)/shard_map/gated_conv/pallas_call | solution.py:426
  96.9 0.6 copy.20
  97.5 0.6 copy.21
  98.2 1.3 %copy.22 = bf16[1,1,8,8,128,128]{5,4,3,2,1,0:T(8,128)(2,1)} copy(bf16[1,1,8,8,128,128]{5,4,3,2,1,0:T(8,128)(2,1)S(1)} %get-tuple-element.8) | data formatting | bytes 4194304
Async XLA Ops:
  2.0 1.6 %copy-start = (bf16[1,1,8,8,128,128]{5,4,3,2,1,0:T(8,128)(2,1)S(1)}, bf16[1,1,8,8,128,128]{5,4,3,2,1,0:T(8,128)(2,1)}, u32[]{:S(2)}) copy-start(bf16[1,1,8,8,128,128]{5,4,3,2,1,0:T(8,128)(2,1)} %feat_hbm.1) | copy-start | bytes 6291460
  3.6 1.0 %copy-start.1 = (s32[1,1,8,128,128]{4,3,2,1,0:T(8,128)S(1)}, s32[1,1,8,128,128]{4,3,2,1,0:T(8,128)}, u32[]{:S(2)}) copy-start(s32[1,1,8,128,128]{4,3,2,1,0:T(8,128)} %mask_hbm.1) | copy-start | bytes 1572868
  4.7 0.9 copy-start.2
  5.6 0.9 copy-start.3
  6.5 0.7 copy-start.4
  7.2 0.7 copy-start.5
  7.9 0.7 copy-start.6
  8.6 0.7 copy-start.7
  9.3 0.7 copy-start.8
  10.0 0.7 copy-start.9

commit v2 on v1

--- a/solution.py
+++ b/solution.py
@@ -36,10 +36,11 @@
 
 def kernel(
     shape,
-    scale_ref, pair_ref, count_ref,
-    h_ref, cot_ref, wet_ref, wtt_ref, gain_ref,
+    scale_hbm, pair_hbm, count_hbm,
+    h_hbm, cot_hbm, wet_hbm, wtt_hbm, gain_hbm,
     wself_hbm, wvalue_hbm, feat_hbm, mask_hbm,
     out_ref, grad_ref, edge_hbm,
+    scale_ref, pair_ref, count_ref, h_ref, cot_ref, wet_ref, wtt_ref, gain_ref,
     wself, wvalue, feat, mask, hbuf, tbuf, gate32, gate16, vmask, nt, onehot, spread,
     send0, send1, recv0, recv1, dbuf, dnt, egbuf, pt, wproj, lut, dtbuf,
     dpart, rcore, s1, rx, s2, ry, dtsend, dtrecv,
@@ -75,6 +76,15 @@
             device_id=device, device_id_type=MESH,
         )
 
+    small = [
+        pltpu.make_async_copy(a, b, lsem.at[4 + i])
+        for i, (a, b) in enumerate((
+            (h_hbm, h_ref), (wtt_hbm, wtt_ref), (wet_hbm, wet_ref), (pair_hbm, pair_ref),
+            (count_hbm, count_ref), (scale_hbm, scale_ref), (cot_hbm, cot_ref), (gain_hbm, gain_ref),
+        ))
+    ]
+    for load in small:
+        load.start()
     loads = [
         pltpu.make_async_copy(wvalue_hbm, wvalue, lsem.at[0]),
         pltpu.make_async_copy(wself_hbm, wself, lsem.at[1]),
@@ -93,6 +103,8 @@
         pl.semaphore_signal(barrier, inc=1, device_id=at_z(lax.rem(z + d, nz)), device_id_type=MESH)
     pl.semaphore_signal(barrier, inc=1, device_id=sibling, device_id_type=MESH)
 
+    for load in small:
+        load.wait()
     h = h_ref[...]
     hbuf[x, y, c] = h
     wtt = jnp.concatenate([wtt_ref[...].astype(F32), jnp.zeros((TB - HEADS, D), F32)], axis=0).astype(LOW)
@@ -102,14 +114,28 @@
 
     pl.semaphore_wait(barrier, ny + nx + nz - 2)
 
-    for d in range(1, ny):
+    near = sorted(range(1, ny), key=lambda d: (min(d, ny - d), d))
+    nearx = sorted(range(1, nx), key=lambda d: (min(d, nx - d), d))
+    farz = sorted(range(1, nz), key=lambda d: (-min(d, nz - d), d))
+    for d in near:
         remote(h_ref, hbuf.at[x, y, c], ysend.at[d], yrecv.at[d], at_y(lax.rem(y + d, ny))).start()
-    for d in range(1, nz):
+    for d in farz:
         remote(tbuf.at[z], tbuf.at[z], tsend.at[d], trecv.at[d], at_z(lax.rem(z + d, nz))).start()
 
+    def block_out(d):
+        v = lax.rem(y + ny - d, ny)
+        block = hbuf.at[x, v, c]
+        if d:
+            remote(block, block, ysend.at[d], yrecv.at[d], at_y(v)).wait_recv()
+        for e in reversed(nearx):
+            remote(block, block, xsend.at[e, d], xrecv.at[e, d], at_x(lax.rem(x + e, nx))).start()
+        remote(block, block, csend.at[0, d], crecv.at[0, d], sibling).start()
+
+    block_out(0)
+
     count = count_ref[0, 0]
-    rows = [jnp.clip(pair_ref[0, 0, t, 0], 0, rb - 1) for t in range(slots)]
-    cols = [jnp.clip(pair_ref[0, 0, t, 1], 0, cb - 1) for t in range(slots)]
+    rows = [jnp.clip(pair_ref[0, 0, 0, t], 0, rb - 1) for t in range(slots)]
+    cols = [jnp.clip(pair_ref[0, 0, 1, t], 0, cb - 1) for t in range(slots)]
     live = [jnp.where(count > t, 1.0, 0.0).astype(F32) for t in range(slots)]
 
     def fill_lut(q, carry):
@@ -136,24 +162,24 @@
     loads[1].wait()
     self_pre = mm(h, wself[...])
 
-    for d in range(1, ny):
+    for d in near:
+        block_out(d)
+    for d in [0] + near:
         v = lax.rem(y + ny - d, ny)
-        remote(hbuf.at[x, v, c], hbuf.at[x, v, c], ysend.at[d], yrecv.at[d], at_y(v)).wait_recv()
-    for d in range(1, nx):
-        remote(hbuf.at[x, :, c], hbuf.at[x, :, c], xsend.at[d], xrecv.at[d], at_x(lax.rem(x + d, nx))).start()
-    remote(hbuf.at[x, :, c], hbuf.at[x, :, c], csend.at[0], crecv.at[0], sibling).start()
-    for d in range(1, nx):
-        v = lax.rem(x + nx - d, nx)
-        remote(hbuf.at[v, :, c], hbuf.at[v, :, c], xsend.at[d], xrecv.at[d], at_x(v)).wait_recv()
-        remote(hbuf.at[v, :, c], hbuf.at[v, :, c], csend.at[d], crecv.at[d], sibling).start()
+        for e in nearx:
+            block = hbuf.at[lax.rem(x + nx - e, nx), v, c]
+            remote(block, block, xsend.at[e, d], xrecv.at[e, d], sibling).wait_recv()
+            remote(block, block, csend.at[e, d], crecv.at[e, d], sibling).start()
     for d in range(1, nz):
         v = lax.rem(z + nz - d, nz)
         remote(tbuf.at[v], tbuf.at[v], tsend.at[d], trecv.at[d], at_z(v)).wait_recv()
     loads[2].wait()
     loads[3].wait()
-    for d in range(nx):
-        v = lax.rem(x + nx - d, nx)
-        remote(hbuf.at[v, :, 1 - c], hbuf.at[v, :, 1 - c], csend.at[d], crecv.at[d], sibling).wait_recv()
+    for d in [0] + near:
+        v = lax.rem(y + ny - d, ny)
+        for e in [0] + nearx:
+            block = hbuf.at[lax.rem(x + nx - e, nx), v, 1 - c]
+            remote(block, block, csend.at[e, d], crecv.at[e, d], sibling).wait_recv()
 
     def h_tile(col):
         per = cbx
@@ -163,8 +189,8 @@
         return hbuf[xi, pl.ds(q * step, step)].reshape(TB, D)
 
     def tile_scalars(t):
-        row = jnp.clip(pair_ref[0, 0, t, 0], 0, rb - 1)
-        col = jnp.clip(pair_ref[0, 0, t, 1], 0, cb - 1)
+        row = jnp.clip(pair_ref[0, 0, 0, t], 0, rb - 1)
+        col = jnp.clip(pair_ref[0, 0, 1, t], 0, cb - 1)
         return row, col, jnp.where(count > t, 1.0, 0.0).astype(F32)
 
     lane_d = iota((TB, D), 1) // SH
@@ -215,7 +241,7 @@
     forward(0)
     for r, total in row_sums(TB, [(0, 0)]):
         send0[r * per:(r + 1) * per] = total.astype(LOW).reshape(per, nd, TB)
-    for d in range(1, nz):
+    for d in farz:
         v = lax.rem(z + d, nz)
         remote(send0.at[v], recv0.at[d], z0send.at[d], z0recv.at[d], at_z(v)).start()
     forward(1)
@@ -223,7 +249,7 @@
         send1[r * per:(r + 1) * per, :, 0:TB] = total.astype(LOW).reshape(per, nd, TB)
     for r, total in row_sums(TB, [(0, TB), (1, TB)]):
         send1[r * per:(r + 1) * per, :, TB:D] = total.astype(LOW).reshape(per, nd, TB)
-    for d in range(1, nz):
+    for d in farz:
         v = lax.rem(z + d, nz)
         remote(send1.at[v], recv1.at[d], z1send.at[d], z1recv.at[d], at_z(v)).start()
 
@@ -264,7 +290,7 @@
     collect = jnp.where(iota((D, TB), 0) // SH == iota((D, TB), 1), 1.0, 0.0).astype(F32)
     dden = -mm_exact(dpre * num, collect) / (floor * floor)
     dbuf[z] = jnp.concatenate([dpre / floor_d, dden], axis=1).astype(LOW)
-    for d in range(1, nz):
+    for d in farz:
         remote(dbuf.at[z], dbuf.at[z], dsend.at[d], drecv.at[d], at_z(lax.rem(z + d, nz))).start()
     own_grad = cot + mm_nt(dpre.astype(LOW), wself[...])
     for d in range(1, nz):
@@ -280,69 +306,98 @@
         dn = dbuf[pl.ds(row * per, per)].reshape(TB, D + TB)
         dnr = dnt[row]
         grads = []
-        dt = jnp.zeros((TB, TB), F32)
         sums = []
         for half in range(2):
             lhs = jnp.concatenate([dn[:, half * TB:(half + 1) * TB], dn[:, D:D + TB]], axis=1)
             rhs = jnp.concatenate([vmask[t, half], onehot[half]], axis=1)
             dsig = mm_nt(lhs, rhs)
+            for k in range(HALF):
+                kk = half * HALF + k
+                dl = dsig[:, k * TB:(k + 1) * TB] * gate32[t, kk]
+                gate32[t, kk] = dl
+                sums.append(jnp.sum(dl, axis=0, keepdims=True))
+                grads.append(mm(dnr[kk * SH:(kk + 1) * SH, :], gate16[t, kk]))
+        stack = jnp.concatenate(grads + sums + [jnp.zeros((TB - HEADS, TB), F32)], axis=0).astype(LOW)
+        pt[t] = mm(wproj[...], stack).T
+        return carry
+
+    lax.fori_loop(0, slots, backward, 0)
+
+    span = ny // cbx
+    home = y // span
+    turn = sorted(range(cbx), key=lambda o: (-min(o, cbx - o), o))
+
+    def column(m, i):
+        def one(xi, carry):
+            block = xi * cbx + m
+            total = pt[lut[block, 0]]
+            for r in range(1, rb):
+                total += pt[lut[block, r]]
+            dpart[xi, pl.ds(m * span, span)] = total.astype(LOW).reshape(span, 2, nd, D)
+            return carry
+
+        lax.fori_loop(0, nx, one, 0)
+        part = pl.ds(m * span, span)
+        remote(
+            dpart.at[:, part, 1 - c], rcore.at[:, part], bcsend.at[i], bcrecv.at[i], sibling
+        ).start()
+
+    for i, o in enumerate(turn):
+        column(lax.rem(home + o, cbx), i)
+    for i, o in enumerate(turn):
+        m = lax.rem(home + o, cbx)
+        part = pl.ds(m * span, span)
+        remote(rcore.at[:, part], rcore.at[:, part], bcsend.at[i], bcrecv.at[i], sibling).wait_recv()
+        s1[:, part] = (dpart[:, part, c].astype(F32) + rcore[:, part].astype(F32)).astype(LOW)
+        for j in range(span):
+            v = m * span + j
+            for e in reversed(nearx):
+                w = lax.rem(x + e, nx)
+                remote(
+                    s1.at[w, v], rx.at[e, v], bxsend.at[e, i * span + j], bxrecv.at[e, i * span + j], at_x(w)
+                ).start()
+
+    def edges(t, carry):
+        dt = jnp.zeros((TB, TB), F32)
+        for half in range(2):
             lows = []
             for k in range(HALF):
                 kk = half * HALF + k
-                dl = dsig[:, k * TB:(k + 1) * TB] * gate32[t, kk]
+                dl = gate32[t, kk]
                 egbuf[t, kk] = (dl * scale_ref[kk]).astype(LOW)
-                sums.append(jnp.sum(dl, axis=0, keepdims=True))
                 lows.append(dl.astype(LOW))
-                grads.append(mm(dnr[kk * SH:(kk + 1) * SH, :], gate16[t, kk]))
             dt += mm(jnp.concatenate(lows, axis=1), onehot[half])
         dtbuf[t] = dt
         pltpu.make_async_copy(egbuf.at[t], edge_hbm.at[0, 0, t], esem.at[t]).start()
-        stack = jnp.concatenate(grads + sums + [jnp.zeros((TB - HEADS, TB), F32)], axis=0).astype(LOW)
-        pt[t] = mm(wproj[...], stack).T
         return carry
 
-    lax.fori_loop(0, slots, backward, 0)
-
+    lax.fori_loop(0, slots, edges, 0)
     for r in range(rb):
         total = jnp.zeros((TB, TB), F32)
         for t in range(slots):
             total += dtbuf[t] * jnp.where(rows[t] == r, 1.0, 0.0).astype(F32)
         dtsend[r * per:(r + 1) * per] = total.astype(LOW).reshape(per, nd, TB)
-
-    def quarter(xi):
-        def one(q, carry):
-            block = xi * cbx + q
-            total = pt[lut[block, 0]]
-            for r in range(1, rb):
-                total += pt[lut[block, r]]
-            step = ny // cbx
-            dpart[xi, pl.ds(q * step, step)] = total.astype(LOW).reshape(step, 2, nd, D)
-            return carry
-
-        lax.fori_loop(0, cbx, one, 0)
-
-    for d in range(nx):
-        v = lax.rem(x + 1 + d, nx)
-        quarter(v)
-        remote(dpart.at[v, :, 1 - c], rcore.at[v], bcsend.at[d], bcrecv.at[d], sibling).start()
-        if d == 0:
-            for e in range(1, nz):
-                w = lax.rem(z + e, nz)
-                remote(dtsend.at[w], dtrecv.at[e], gsend.at[e], grecv.at[e], at_z(w)).start()
-    for d in range(nx):
-        v = lax.rem(x + 1 + d, nx)
-        remote(rcore.at[v], rcore.at[v], bcsend.at[d], bcrecv.at[d], sibling).wait_recv()
-        s1[v] = (dpart[v, :, c].astype(F32) + rcore[v].astype(F32)).astype(LOW)
-        if d < nx - 1:
-            remote(s1.at[v], rx.at[d], bxsend.at[d], bxrecv.at[d], at_x(v)).start()
-    total = s1[x].astype(F32)
-    for d in range(nx - 1):
-        remote(rx.at[d], rx.at[d], bxsend.at[d], bxrecv.at[d], at_x(x)).wait_recv()
-        total += rx[d].astype(F32)
-    s2[...] = total.astype(LOW)
-    for d in range(1, ny):
-        v = lax.rem(y + d, ny)
-        remote(s2.at[v], ry.at[d], bysend.at[d], byrecv.at[d], at_y(v)).start()
+    for e in farz:
+        w = lax.rem(z + e, nz)
+        remote(dtsend.at[w], dtrecv.at[e], gsend.at[e], grecv.at[e], at_z(w)).start()
+
+    for i, o in enumerate(turn):
+        m = lax.rem(home + o, cbx)
+        for j in range(span):
+            v = m * span + j
+            total = s1[x, v].astype(F32)
+            for e in nearx:
+                remote(
+                    rx.at[e, v], rx.at[e, v], bxsend.at[e, i * span + j], bxrecv.at[e, i * span + j], sibling
+                ).wait_recv()
+                total += rx[e, v].astype(F32)
+            s2[v] = total.astype(LOW)
+
+            @pl.when(v != y)
+            def _():
+                n = lax.rem(y + ny - v, ny)
+                remote(s2.at[v], ry.at[n], bysend.at[n], byrecv.at[n], at_y(v)).start()
+
     dt = dtsend[z].astype(F32)
     for d in range(1, nz):
         remote(dtrecv.at[d], dtrecv.at[d], gsend.at[d], grecv.at[d], at_z(z)).wait_recv()
@@ -355,22 +410,40 @@
     grad_ref[...] = own_grad + final
 
     for d in range(1, ny):
-        remote(h_ref, h_ref, ysend.at[d], yrecv.at[d], at_y(y)).wait_send()
-        remote(s2.at[y], s2.at[y], bysend.at[d], byrecv.at[d], at_y(y)).wait_send()
-    for d in range(1, nx):
-        remote(hbuf.at[x, :, c], hbuf.at[x, :, c], xsend.at[d], xrecv.at[d], at_x(x)).wait_send()
-        remote(s1.at[x], s1.at[x], bxsend.at[d - 1], bxrecv.at[d - 1], at_x(x)).wait_send()
-    for d in range(nx):
-        remote(hbuf.at[x, :, c], hbuf.at[x, :, c], csend.at[d], crecv.at[d], sibling).wait_send()
-        remote(rcore.at[x], rcore.at[x], bcsend.at[d], bcrecv.at[d], sibling).wait_send()
-    for d in range(1, nz):
-        remote(tbuf.at[z], tbuf.at[z], tsend.at[d], trecv.at[d], at_z(z)).wait_send()
-        remote(send0.at[z], send0.at[z], z0send.at[d], z0recv.at[d], at_z(z)).wait_send()
-        remote(send1.at[z], send1.at[z], z1send.at[d], z1recv.at[d], at_z(z)).wait_send()
-        remote(dbuf.at[z], dbuf.at[z], dsend.at[d], drecv.at[d], at_z(z)).wait_send()
-        remote(dtsend.at[z], dtsend.at[z], gsend.at[d], grecv.at[d], at_z(z)).wait_send()
+        remote(h_ref, h_ref, ysend.at[d], yrecv.at[d], sibling).wait_send()
+        remote(s2.at[y], s2.at[y], bysend.at[d], byrecv.at[d], sibling).wait_send()
+    for d in range(ny):
+        for e in range(1, nx):
+            remote(h_ref, h_ref, xsend.at[e, d], xrecv.at[e, d], sibling).wait_send()
+            remote(s2.at[y], s2.at[y], bxsend.at[e, d], bxrecv.at[e, d], sibling).wait_send()
+        for e in range(nx):
+            remote(h_ref, h_ref, csend.at[e, d], crecv.at[e, d], sibling).wait_send()
+    for i in range(cbx):
+        part = pl.ds(i * span, span)
+        remote(rcore.at[:, part], rcore.at[:, part], bcsend.at[i], bcrecv.at[i], sibling).wait_send()
+    for d in range(1, nz):
+        remote(tbuf.at[z], tbuf.at[z], tsend.at[d], trecv.at[d], sibling).wait_send()
+        remote(send0.at[z], send0.at[z], z0send.at[d], z0recv.at[d], sibling).wait_send()
+        remote(send1.at[z], send1.at[z], z1send.at[d], z1recv.at[d], sibling).wait_send()
+        remote(dbuf.at[z], dbuf.at[z], dsend.at[d], drecv.at[d], sibling).wait_send()
+        remote(dtsend.at[z], dtsend.at[z], gsend.at[d], grecv.at[d], sibling).wait_send()
     for t in range(slots):
         pltpu.make_async_copy(egbuf.at[t], edge_hbm.at[0, 0, t], esem.at[t]).wait()
+
+
+def flush_kernel(out_ref, grad_ref, edge_ref, out_hbm, grad_hbm, edge_hbm, out, grad, edge, isem, osem):
+    slots = edge.shape[0]
+    pairs = [(edge_ref.at[0, 0, t], edge.at[t], edge_hbm.at[0, 0, t]) for t in range(slots)]
+    pairs += [(out_ref, out, out_hbm), (grad_ref, grad, grad_hbm)]
+    reads = [pltpu.make_async_copy(a, b, isem.at[i]) for i, (a, b, _) in enumerate(pairs)]
+    writes = [pltpu.make_async_copy(b, c, osem.at[i]) for i, (_, b, c) in enumerate(pairs)]
+    for copy in reads:
+        copy.start()
+    for read, write in zip(reads, writes):
+        read.wait()
+        write.start()
+    for copy in writes:
+        copy.wait()
 
 
 def body(
@@ -383,10 +456,19 @@
     slots = edge_mask.shape[2]
     rb = nz * nd // TB
     cb = nx * ny * 2 * nd // TB
+    cbx = cb // nx
     vmem = pl.BlockSpec(memory_space=pltpu.VMEM)
-    smem = pl.BlockSpec(memory_space=pltpu.SMEM)
-    hbm = pl.BlockSpec(memory_space=pl.ANY)
+    hbm = pl.BlockSpec(memory_space=pltpu.HBM)
+    free = pl.BlockSpec(memory_space=pl.ANY)
     scratch = [
+        pltpu.SMEM((HEADS,), F32),
+        pltpu.SMEM((1, 1, 2, slots), jnp.int32),
+        pltpu.SMEM((1, 1), jnp.int32),
+        pltpu.VMEM((nd, D), LOW),
+        pltpu.VMEM((nd, D), LOW),
+        pltpu.VMEM((HEADS, D), LOW),
+        pltpu.VMEM((HEADS, D), LOW),
+        pltpu.VMEM((1, D), F32),
         pltpu.VMEM((D, D), LOW),
         pltpu.VMEM((D, D), LOW),
         pltpu.VMEM((slots, HEADS, TB, TB), LOW),
@@ -418,30 +500,48 @@
         pltpu.VMEM((ny, nd, D), LOW),
         pltpu.VMEM((nz, nd, TB), LOW),
         pltpu.VMEM((nz, nd, TB), LOW),
-        pltpu.SemaphoreType.DMA((4,)),
+        pltpu.SemaphoreType.DMA((12,)),
         pltpu.SemaphoreType.DMA((slots,)),
     ]
-    for n in (ny, nx, nx, nz, nz, nz, nz, nx, nx, ny, nz):
-        scratch += [pltpu.SemaphoreType.DMA((n,)), pltpu.SemaphoreType.DMA((n,))]
-    return pl.pallas_call(
+    for n in (
+        (ny,), (nx, ny), (nx, ny), (nz,), (nz,), (nz,), (nz,), (cbx,), (nx, ny), (ny,), (nz,)
+    ):
+        scratch += [pltpu.SemaphoreType.DMA(n), pltpu.SemaphoreType.DMA(n)]
+    shapes = (
+        jax.ShapeDtypeStruct((nd, D), LOW),
+        jax.ShapeDtypeStruct((nd, D), F32),
+        jax.ShapeDtypeStruct((1, 1, slots, HEADS, TB, TB), LOW),
+    )
+    results = pl.pallas_call(
         functools.partial(kernel, (nx, ny, nz, nd, slots)),
-        out_shape=(
-            jax.ShapeDtypeStruct((nd, D), LOW),
-            jax.ShapeDtypeStruct((nd, D), F32),
-            jax.ShapeDtypeStruct((1, 1, slots, HEADS, TB, TB), LOW),
-        ),
-        in_specs=[smem, smem, smem, vmem, vmem, vmem, vmem, vmem, hbm, hbm, hbm, hbm],
-        out_specs=(vmem, vmem, hbm),
+        out_shape=shapes,
+        in_specs=[hbm] * 12,
+        out_specs=(vmem, vmem, free),
         scratch_shapes=scratch,
         compiler_params=pltpu.CompilerParams(
-            collective_id=0, has_side_effects=True, vmem_limit_bytes=48 * 1024 * 1024
+            collective_id=0, has_side_effects=True, vmem_limit_bytes=64 * 1024 * 1024
         ),
         name="gated_conv",
     )(
-        edge_scale, tile_index, tile_count,
+        edge_scale, tile_index.transpose(0, 1, 3, 2), tile_count,
         node_hidden_state, cotangent, weight_edge.T, weight_target.T, layer_norm_gain[None, :],
         self_projection_weight, weight_value, edge_feature, edge_mask,
     )
+    return pl.pallas_call(
+        flush_kernel,
+        out_shape=shapes,
+        in_specs=[free] * 3,
+        out_specs=(hbm, hbm, hbm),
+        scratch_shapes=[
+            pltpu.VMEM((nd, D), LOW),
+            pltpu.VMEM((nd, D), F32),
+            pltpu.VMEM((slots, HEADS, TB, TB), LOW),
+            pltpu.SemaphoreType.DMA((slots + 2,)),
+            pltpu.SemaphoreType.DMA((slots + 2,)),
+        ],
+        compiler_params=pltpu.CompilerParams(vmem_limit_bytes=64 * 1024 * 1024),
+        name="flush",
+    )(*results)
 
 
 def build(mesh, nx, ny):

time: 99.9 us -> 83.5 us (0.84)
  local copies, waits for them, and re-layouts: 11.9 us -> 0 us
  Pallas kernels: 86.3 us -> 82 us
    unnamed x24 -> x0, local copies, waits for them, and re-layouts: 11.9 us -> none
    pallas_call x1, Pallas kernels: 86.3 us -> 79.6 us  [body(): pl.pallas_call(functools.partial(kernel, (nx, ny, nz, nd, slots)), out_sh...]
    pallas_call x0 -> x1, Pallas kernels: none -> 2.44 us  [body(): pl.pallas_call(flush_kernel, out_shape=shapes, in_specs=[free] * 3, out_s...]
where the time goes in v2:
time: 83.5 us; the launch traced here: 83.3 us
  Pallas kernels  82 us (98%)
  between operations  1.29 us (2%)
    pallas_call x1, Pallas kernels, body(): pl.pallas_call(functools.partial(kernel, (nx, ny, nz, nd, slots)), out_sh...  79.6 us
    pallas_call x1, Pallas kernels, body(): pl.pallas_call(flush_kernel, out_shape=shapes, in_specs=[free] * 3, out_s...  2.44 us

profile of v2, /device:TPU:1, one launch (start us, length us, event | category | flops | bytes accessed | tf_op | source)
XLA Modules:
  0.0 83.3 jit_solution(11816545801353149284)
XLA Ops:
  1.3 79.6 %gated_conv.1 = (bf16[32,256]{1,0:T(8,128)(2,1)}, f32[32,256]{1,0:T(8,128)}, bf16[1,1,8,8,128,128]{5,4,3,2,1,0:T(8,128)(2,1)}) custom-call(f32[8]{0:T(128)} %scale_hbm.1, s32[1,1,2,8]{3,2,1,0:T(2,128)} %bitcast.6, s32[1,1]{1,0:T(1,128)S(6)} %copy.15.count_hbm, bf16[32,256]{1,0:T(8,128)(2,1)} %h_hbm.1, bf16[32,256]{1,0:T(8,128)(2,1)} %cot_hbm.1, ...), custom_call_target="tpu_custom_call" | custom-call | tf_op jit(solution)/shard_map/gated_conv/pallas_call | solution.py:515
  80.8 2.4 %flush.1 = (bf16[32,256]{1,0:T(8,128)(2,1)}, f32[32,256]{1,0:T(8,128)}, bf16[1,1,8,8,128,128]{5,4,3,2,1,0:T(8,128)(2,1)}) custom-call(bf16[32,256]{1,0:T(8,128)(2,1)} %get-tuple-element.6.out_ref, f32[32,256]{1,0:T(8,128)} %get-tuple-element.7.grad_ref, bf16[1,1,8,8,128,128]{5,4,3,2,1,0:T(8,128)(2,1)} %get-tuple-element.8.edge_ref), custom_call_target="tpu_custom_call" | custom-call | tf_op jit(solution)/shard_map/flush/pallas_call | solution.py:530

commit v3 on v2

--- a/solution.py
+++ b/solution.py
@@ -12,6 +12,10 @@
 D = 256
 HEADS = 8
 HALF = 4
+UP = 4
+UF = 4
+UB = 4
+UE = 4
 TB = 128
 SH = D // HEADS
 MESH = pl.DeviceIdType.MESH
@@ -41,8 +45,8 @@
     wself_hbm, wvalue_hbm, feat_hbm, mask_hbm,
     out_ref, grad_ref, edge_hbm,
     scale_ref, pair_ref, count_ref, h_ref, cot_ref, wet_ref, wtt_ref, gain_ref,
-    wself, wvalue, feat, mask, hbuf, tbuf, gate32, gate16, vmask, nt, onehot, spread,
-    send0, send1, recv0, recv1, dbuf, dnt, egbuf, pt, wproj, lut, dtbuf,
+    wself, wvalue, feat, mask, hbuf, tbuf, gate32, gate16, vmask, vals, vmaskt, srcs, nt, onehot, onehott, spread,
+    send0, send1, recv0, recv1, dbuf, ddbuf, dnt, egbuf, pt, wproj, lut, dtbuf,
     dpart, rcore, s1, rx, s2, ry, dtsend, dtrecv,
     lsem, esem,
     ysend, yrecv, xsend, xrecv, csend, crecv, tsend, trecv,
@@ -129,9 +133,11 @@
             remote(block, block, ysend.at[d], yrecv.at[d], at_y(v)).wait_recv()
         for e in reversed(nearx):
             remote(block, block, xsend.at[e, d], xrecv.at[e, d], at_x(lax.rem(x + e, nx))).start()
-        remote(block, block, csend.at[0, d], crecv.at[0, d], sibling).start()
 
     block_out(0)
+
+    for d in near:
+        block_out(d)
 
     count = count_ref[0, 0]
     rows = [jnp.clip(pair_ref[0, 0, 0, t], 0, rb - 1) for t in range(slots)]
@@ -152,34 +158,31 @@
     for half in range(2):
         for k in range(HALF):
             onehot[half, k * TB:(k + 1) * TB, :] = jnp.where(lane == half * HALF + k, 1.0, 0.0).astype(LOW)
-            spread[half, :, k * TB:(k + 1) * TB] = jnp.where(
-                iota((TB, TB), 0) == half * HALF + k, 0.5, 0.0
-            ).astype(LOW)
+            here = iota((TB, TB), 0) == half * HALF + k
+            spread[half, :, k * TB:(k + 1) * TB] = jnp.where(here, 0.5, 0.0).astype(LOW)
+            onehott[half, :, k * TB:(k + 1) * TB] = jnp.where(here, 1.0, 0.0).astype(LOW)
     pt[slots] = jnp.zeros((TB, D), F32)
     loads[0].wait()
-    wproj[:, 0:D] = wvalue[...]
-    wproj[:, D:D + TB] = wet32.T.astype(LOW)
+    wproj[0:D] = wvalue[...].astype(F32).T.astype(LOW)
+    wproj[D:D + TB] = wet32.astype(LOW)
     loads[1].wait()
     self_pre = mm(h, wself[...])
 
-    for d in near:
-        block_out(d)
     for d in [0] + near:
         v = lax.rem(y + ny - d, ny)
         for e in nearx:
             block = hbuf.at[lax.rem(x + nx - e, nx), v, c]
             remote(block, block, xsend.at[e, d], xrecv.at[e, d], sibling).wait_recv()
-            remote(block, block, csend.at[e, d], crecv.at[e, d], sibling).start()
+        row = hbuf.at[:, v, c]
+        remote(row, row, csend.at[d], crecv.at[d], sibling).start()
     for d in range(1, nz):
         v = lax.rem(z + nz - d, nz)
         remote(tbuf.at[v], tbuf.at[v], tsend.at[d], trecv.at[d], at_z(v)).wait_recv()
     loads[2].wait()
     loads[3].wait()
     for d in [0] + near:
-        v = lax.rem(y + ny - d, ny)
-        for e in [0] + nearx:
-            block = hbuf.at[lax.rem(x + nx - e, nx), v, 1 - c]
-            remote(block, block, csend.at[e, d], crecv.at[e, d], sibling).wait_recv()
+        row = hbuf.at[:, lax.rem(y + ny - d, ny), 1 - c]
+        remote(row, row, csend.at[d], crecv.at[d], sibling).wait_recv()
 
     def h_tile(col):
         per = cbx
@@ -199,20 +202,30 @@
         per = TB // nd
         return tbuf[pl.ds(row * per, per)].reshape(TB, TB)
 
+    def prepare(t, carry):
+        row, col, flag = tile_scalars(t)
+        ht = h_tile(col)
+        val = mm(ht, wvalue[...])
+        vals[t] = val
+        srcs[t] = mm_nt(wet, ht)[:HEADS].astype(LOW).astype(F32) * 0.5
+        for half in range(2):
+            for k in range(HALF):
+                vmask[t, half, k * TB:(k + 1) * TB, :] = jnp.where(
+                    lane // SH == k, val[:, half * TB:(half + 1) * TB], 0.0
+                ).astype(LOW)
+        return carry
+
+    lax.fori_loop(0, slots, prepare, 0, unroll=UP)
+
     def forward(half):
         def step(t, carry):
             row, col, flag = tile_scalars(t)
-            ht = h_tile(col)
-            val = mm(ht, wvalue[:, half * TB:(half + 1) * TB])
-            src = mm_nt(wet, ht).astype(LOW).astype(F32) * 0.5
+            src = srcs[t]
             outer = mm(t_rows(row), spread[half])
             weight = mask[t].astype(F32) * flag
             gates = []
             for k in range(HALF):
                 kk = half * HALF + k
-                vmask[t, half, k * TB:(k + 1) * TB, :] = jnp.where(
-                    lane // SH == k, val, 0.0
-                ).astype(LOW)
                 arg = feat[t, kk].astype(F32) * (scale_ref[kk] * 0.5) + (
                     outer[:, k * TB:(k + 1) * TB] + src[kk:kk + 1, :]
                 )
@@ -225,7 +238,7 @@
             nt[half, t] = mm(jnp.concatenate(gates, axis=1), rhs)
             return carry
 
-        lax.fori_loop(0, slots, step, 0)
+        lax.fori_loop(0, slots, step, 0, unroll=UF)
 
     per = TB // nd
 
@@ -246,9 +259,12 @@
         remote(send0.at[v], recv0.at[d], z0send.at[d], z0recv.at[d], at_z(v)).start()
     forward(1)
     for r, total in row_sums(TB, [(1, 0)]):
-        send1[r * per:(r + 1) * per, :, 0:TB] = total.astype(LOW).reshape(per, nd, TB)
+        send1[r * per:(r + 1) * per, 0:nd] = total.astype(LOW).reshape(per, nd, TB)
     for r, total in row_sums(TB, [(0, TB), (1, TB)]):
-        send1[r * per:(r + 1) * per, :, TB:D] = total.astype(LOW).reshape(per, nd, TB)
+        total = total.reshape(per, 2, nd // 2, TB)
+        moved = pltpu.roll(total[:, 1].reshape(TB // 2, TB), HEADS, axis=1)
+        packed = total[:, 0].reshape(TB // 2, TB) + moved
+        send1[r * per:(r + 1) * per, nd:] = packed.astype(LOW).reshape(per, nd // 2, TB)
     for d in farz:
         v = lax.rem(z + d, nz)
         remote(send1.at[v], recv1.at[d], z1send.at[d], z1recv.at[d], at_z(v)).start()
@@ -257,6 +273,12 @@
         for k in range(HEADS):
             g = gate32[t, k]
             gate32[t, k] = g - g * g
+        for half in range(2):
+            turned = vals[t, :, half * TB:(half + 1) * TB].T
+            for k in range(HALF):
+                vmaskt[t, half, :, k * TB:(k + 1) * TB] = jnp.where(
+                    iota((TB, TB), 0) // SH == k, turned, 0.0
+                ).astype(LOW)
         return carry
 
     lax.fori_loop(0, slots, slope, 0)
@@ -270,8 +292,8 @@
         remote(recv1.at[d], recv1.at[d], z1send.at[d], z1recv.at[d], at_z(z)).wait_recv()
         both += recv1[d].astype(F32)
 
-    num = jnp.concatenate([num0, both[:, 0:TB]], axis=1)
-    floor = both[:, TB:D] + 1.0
+    num = jnp.concatenate([num0, both[0:nd]], axis=1)
+    floor = jnp.concatenate([both[nd:], pltpu.roll(both[nd:], TB - HEADS, axis=1)], axis=0) + 1.0
     expand = jnp.where(iota((TB, D), 0) == lane_d, 1.0, 0.0).astype(F32)
     floor_d = mm_exact(floor, expand)
     pre = self_pre + num / floor_d
@@ -289,7 +311,10 @@
     )
     collect = jnp.where(iota((D, TB), 0) // SH == iota((D, TB), 1), 1.0, 0.0).astype(F32)
     dden = -mm_exact(dpre * num, collect) / (floor * floor)
-    dbuf[z] = jnp.concatenate([dpre / floor_d, dden], axis=1).astype(LOW)
+    dnum = dpre / floor_d
+    dbuf[z] = jnp.concatenate(
+        [dnum[:, :TB], dnum[:, TB:], dden[:nd // 2] + pltpu.roll(dden[nd // 2:], HEADS, axis=1)], axis=0
+    ).astype(LOW)
     for d in farz:
         remote(dbuf.at[z], dbuf.at[z], dsend.at[d], drecv.at[d], at_z(lax.rem(z + d, nz))).start()
     own_grad = cot + mm_nt(dpre.astype(LOW), wself[...])
@@ -298,30 +323,35 @@
         remote(dbuf.at[v], dbuf.at[v], dsend.at[d], drecv.at[d], at_z(v)).wait_recv()
 
     for r in range(rb):
-        block = dbuf[r * per:(r + 1) * per, :, 0:D].reshape(TB, D).astype(F32)
-        dnt[r] = block.T.astype(LOW)
+        for half in range(2):
+            block = dbuf[r * per:(r + 1) * per, half * nd:(half + 1) * nd].reshape(TB, TB)
+            dnt[r, half * TB:(half + 1) * TB] = block.astype(F32).T.astype(LOW)
+    packed = dbuf[:, 2 * nd:].astype(F32).reshape(nz * nd // 2, TB)
+    ddbuf[:, :nd // 2] = packed.astype(LOW).reshape(nz, nd // 2, TB)
+    ddbuf[:, nd // 2:] = pltpu.roll(packed, TB - HEADS, axis=1).astype(LOW).reshape(nz, nd // 2, TB)
 
     def backward(t, carry):
         row, col, flag = tile_scalars(t)
-        dn = dbuf[pl.ds(row * per, per)].reshape(TB, D + TB)
+        dd = ddbuf[pl.ds(row * per, per)].reshape(TB, TB)
         dnr = dnt[row]
         grads = []
         sums = []
         for half in range(2):
-            lhs = jnp.concatenate([dn[:, half * TB:(half + 1) * TB], dn[:, D:D + TB]], axis=1)
-            rhs = jnp.concatenate([vmask[t, half], onehot[half]], axis=1)
-            dsig = mm_nt(lhs, rhs)
+            dn = dbuf[pl.ds(row * per, per), half * nd:(half + 1) * nd].reshape(TB, TB)
+            lhs = jnp.concatenate([dn, dd], axis=1)
+            rhs = jnp.concatenate([vmaskt[t, half], onehott[half]], axis=0)
+            dsig = mm(lhs, rhs)
             for k in range(HALF):
                 kk = half * HALF + k
                 dl = dsig[:, k * TB:(k + 1) * TB] * gate32[t, kk]
                 gate32[t, kk] = dl
                 sums.append(jnp.sum(dl, axis=0, keepdims=True))
                 grads.append(mm(dnr[kk * SH:(kk + 1) * SH, :], gate16[t, kk]))
-        stack = jnp.concatenate(grads + sums + [jnp.zeros((TB - HEADS, TB), F32)], axis=0).astype(LOW)
-        pt[t] = mm(wproj[...], stack).T
+        stack = jnp.concatenate(grads + sums + [jnp.zeros((TB - HEADS, TB), F32)], axis=0)
+        pt[t] = mm(stack.T.astype(LOW), wproj[...])
         return carry
 
-    lax.fori_loop(0, slots, backward, 0)
+    lax.fori_loop(0, slots, backward, 0, unroll=UB)
 
     span = ny // cbx
     home = y // span
@@ -371,7 +401,7 @@
         pltpu.make_async_copy(egbuf.at[t], edge_hbm.at[0, 0, t], esem.at[t]).start()
         return carry
 
-    lax.fori_loop(0, slots, edges, 0)
+    lax.fori_loop(0, slots, edges, 0, unroll=UE)
     for r in range(rb):
         total = jnp.zeros((TB, TB), F32)
         for t in range(slots):
@@ -416,8 +446,8 @@
         for e in range(1, nx):
             remote(h_ref, h_ref, xsend.at[e, d], xrecv.at[e, d], sibling).wait_send()
             remote(s2.at[y], s2.at[y], bxsend.at[e, d], bxrecv.at[e, d], sibling).wait_send()
-        for e in range(nx):
-            remote(h_ref, h_ref, csend.at[e, d], crecv.at[e, d], sibling).wait_send()
+        row = hbuf.at[:, y, c]
+        remote(row, row, csend.at[d], crecv.at[d], sibling).wait_send()
     for i in range(cbx):
         part = pl.ds(i * span, span)
         remote(rcore.at[:, part], rcore.at[:, part], bcsend.at[i], bcrecv.at[i], sibling).wait_send()
@@ -478,18 +508,23 @@
         pltpu.VMEM((slots, HEADS, TB, TB), F32),
         pltpu.VMEM((slots, HEADS, TB, TB), LOW),
         pltpu.VMEM((slots, 2, HALF * TB, TB), LOW),
+        pltpu.VMEM((slots, TB, D), F32),
+        pltpu.VMEM((slots, 2, TB, HALF * TB), LOW),
+        pltpu.VMEM((slots, HEADS, TB), F32),
         pltpu.VMEM((2, slots, TB, D), F32),
         pltpu.VMEM((2, HALF * TB, TB), LOW),
         pltpu.VMEM((2, TB, HALF * TB), LOW),
+        pltpu.VMEM((2, TB, HALF * TB), LOW),
         pltpu.VMEM((nz, nd, TB), LOW),
-        pltpu.VMEM((nz, nd, D), LOW),
+        pltpu.VMEM((nz, nd + nd // 2, TB), LOW),
         pltpu.VMEM((nz, nd, TB), LOW),
-        pltpu.VMEM((nz, nd, D), LOW),
-        pltpu.VMEM((nz, nd, D + TB), LOW),
+        pltpu.VMEM((nz, nd + nd // 2, TB), LOW),
+        pltpu.VMEM((nz, 2 * nd + nd // 2, TB), LOW),
+        pltpu.VMEM((nz, nd, TB), LOW),
         pltpu.VMEM((rb, D, TB), LOW),
         pltpu.VMEM((slots, HEADS, TB, TB), LOW),
         pltpu.VMEM((slots + 1, TB, D), F32),
-        pltpu.VMEM((D, D + TB), LOW),
+        pltpu.VMEM((D + TB, D), LOW),
         pltpu.SMEM((cb, rb), jnp.int32),
         pltpu.VMEM((slots, TB, TB), F32),
         pltpu.VMEM((nx, ny, 2, nd, D), LOW),
@@ -504,7 +539,7 @@
         pltpu.SemaphoreType.DMA((slots,)),
     ]
     for n in (
-        (ny,), (nx, ny), (nx, ny), (nz,), (nz,), (nz,), (nz,), (cbx,), (nx, ny), (ny,), (nz,)
+        (ny,), (nx, ny), (ny,), (nz,), (nz,), (nz,), (nz,), (cbx,), (nx, ny), (ny,), (nz,)
     ):
         scratch += [pltpu.SemaphoreType.DMA(n), pltpu.SemaphoreType.DMA(n)]
     shapes = (

time: 83.5 us -> 76.7 us (0.919)
  Pallas kernels: 82 us -> 75.2 us
    pallas_call x1, Pallas kernels: 79.6 us -> 72.8 us  [body(): pl.pallas_call(functools.partial(kernel, (nx, ny, nz, nd, slots)), out_sh...]
where the time goes in v3:
time: 76.7 us; the launch traced here: 76.5 us
  Pallas kernels  75.2 us (98%)
  between operations  1.29 us (2%)
    pallas_call x1, Pallas kernels, body(): pl.pallas_call(functools.partial(kernel, (nx, ny, nz, nd, slots)), out_sh...  72.8 us
    pallas_call x1, Pallas kernels, body(): pl.pallas_call(flush_kernel, out_shape=shapes, in_specs=[free] * 3, out_s...  2.44 us

profile of v3, /device:TPU:1, one launch (start us, length us, event | category | flops | bytes accessed | tf_op | source)
XLA Modules:
  0.0 76.5 jit_solution(14880197481312870770)
XLA Ops:
  1.3 72.8 %gated_conv.1 = (bf16[32,256]{1,0:T(8,128)(2,1)}, f32[32,256]{1,0:T(8,128)}, bf16[1,1,8,8,128,128]{5,4,3,2,1,0:T(8,128)(2,1)}) custom-call(f32[8]{0:T(128)} %scale_hbm.1, s32[1,1,2,8]{3,2,1,0:T(2,128)} %bitcast.6, s32[1,1]{1,0:T(1,128)S(6)} %copy.15.count_hbm, bf16[32,256]{1,0:T(8,128)(2,1)} %h_hbm.1, bf16[32,256]{1,0:T(8,128)(2,1)} %cot_hbm.1, ...), custom_call_target="tpu_custom_call" | custom-call | tf_op jit(solution)/shard_map/gated_conv/pallas_call | solution.py:550
  74.1 2.4 %flush.1 = (bf16[32,256]{1,0:T(8,128)(2,1)}, f32[32,256]{1,0:T(8,128)}, bf16[1,1,8,8,128,128]{5,4,3,2,1,0:T(8,128)(2,1)}) custom-call(bf16[32,256]{1,0:T(8,128)(2,1)} %get-tuple-element.6.out_ref, f32[32,256]{1,0:T(8,128)} %get-tuple-element.7.grad_ref, bf16[1,1,8,8,128,128]{5,4,3,2,1,0:T(8,128)(2,1)} %get-tuple-element.8.edge_ref), custom_call_target="tpu_custom_call" | custom-call | tf_op jit(solution)/shard_map/flush/pallas_call | solution.py:565

commit v4 on v3

--- a/solution.py
+++ b/solution.py
@@ -12,9 +12,9 @@
 D = 256
 HEADS = 8
 HALF = 4
-UP = 4
+UP = 8
 UF = 4
-UB = 4
+UB = 8
 UE = 4
 TB = 128
 SH = D // HEADS
@@ -45,12 +45,12 @@
     wself_hbm, wvalue_hbm, feat_hbm, mask_hbm,
     out_ref, grad_ref, edge_hbm,
     scale_ref, pair_ref, count_ref, h_ref, cot_ref, wet_ref, wtt_ref, gain_ref,
-    wself, wvalue, feat, mask, hbuf, tbuf, gate32, gate16, vmask, vals, vmaskt, srcs, nt, onehot, onehott, spread,
-    send0, send1, recv0, recv1, dbuf, ddbuf, dnt, egbuf, pt, wproj, lut, dtbuf,
+    wself, wvalue, feat, mask, hbuf, tbuf, gate32, gatet, vmask, vals, vmaskt, srcs, nt, onehot, onehott, spread,
+    send0, send1, recv0, recv1, dbuf, dbuf1, ddbuf, dnmask, sums, stack, egbuf, pt, wproj, lut, dtbuf,
     dpart, rcore, s1, rx, s2, ry, dtsend, dtrecv,
     lsem, esem,
     ysend, yrecv, xsend, xrecv, csend, crecv, tsend, trecv,
-    z0send, z0recv, z1send, z1recv, dsend, drecv,
+    z0send, z0recv, z1send, z1recv, dsend, drecv, d1send, d1recv,
     bcsend, bcrecv, bxsend, bxrecv, bysend, byrecv, gsend, grecv,
 ):
     nx, ny, nz, nd, slots = shape
@@ -231,9 +231,7 @@
                 )
                 gate = (0.5 * jnp.tanh(arg) + 0.5) * weight
                 gate32[t, kk] = gate
-                low = gate.astype(LOW)
-                gate16[t, kk] = low
-                gates.append(low)
+                gates.append(gate.astype(LOW))
             rhs = jnp.concatenate([vmask[t, half], onehot[half]], axis=1)
             nt[half, t] = mm(jnp.concatenate(gates, axis=1), rhs)
             return carry
@@ -270,13 +268,15 @@
         remote(send1.at[v], recv1.at[d], z1send.at[d], z1recv.at[d], at_z(v)).start()
 
     def slope(t, carry):
-        for k in range(HEADS):
-            g = gate32[t, k]
-            gate32[t, k] = g - g * g
         for half in range(2):
             turned = vals[t, :, half * TB:(half + 1) * TB].T
             for k in range(HALF):
-                vmaskt[t, half, :, k * TB:(k + 1) * TB] = jnp.where(
+                kk = half * HALF + k
+                lanes = slice(k * TB, (k + 1) * TB)
+                g = gate32[t, kk]
+                gate32[t, kk] = g - g * g
+                gatet[t, half, :, lanes] = g.T.astype(LOW)
+                vmaskt[t, half, :, lanes] = jnp.where(
                     iota((TB, TB), 0) // SH == k, turned, 0.0
                 ).astype(LOW)
         return carry
@@ -312,46 +312,60 @@
     collect = jnp.where(iota((D, TB), 0) // SH == iota((D, TB), 1), 1.0, 0.0).astype(F32)
     dden = -mm_exact(dpre * num, collect) / (floor * floor)
     dnum = dpre / floor_d
+    lead = nd + nd // 2
     dbuf[z] = jnp.concatenate(
-        [dnum[:, :TB], dnum[:, TB:], dden[:nd // 2] + pltpu.roll(dden[nd // 2:], HEADS, axis=1)], axis=0
+        [dnum[:, :TB], dden[:nd // 2] + pltpu.roll(dden[nd // 2:], HEADS, axis=1)], axis=0
     ).astype(LOW)
-    for d in farz:
-        remote(dbuf.at[z], dbuf.at[z], dsend.at[d], drecv.at[d], at_z(lax.rem(z + d, nz))).start()
+    dbuf1[z] = dnum[:, TB:].astype(LOW)
+    for part, ssem, rsem in ((dbuf, dsend, drecv), (dbuf1, d1send, d1recv)):
+        for d in farz:
+            block = part.at[z]
+            remote(block, block, ssem.at[d], rsem.at[d], at_z(lax.rem(z + d, nz))).start()
     own_grad = cot + mm_nt(dpre.astype(LOW), wself[...])
-    for d in range(1, nz):
-        v = lax.rem(z + nz - d, nz)
-        remote(dbuf.at[v], dbuf.at[v], dsend.at[d], drecv.at[d], at_z(v)).wait_recv()
-
-    for r in range(rb):
-        for half in range(2):
-            block = dbuf[r * per:(r + 1) * per, half * nd:(half + 1) * nd].reshape(TB, TB)
-            dnt[r, half * TB:(half + 1) * TB] = block.astype(F32).T.astype(LOW)
-    packed = dbuf[:, 2 * nd:].astype(F32).reshape(nz * nd // 2, TB)
+
+    halves = (dbuf, dbuf1)
+
+    def mask_rows(half):
+        for r in range(rb):
+            block = halves[half][r * per:(r + 1) * per, 0:nd].reshape(TB, TB).astype(F32)
+            for k in range(HALF):
+                dnmask[r, half, k * TB:(k + 1) * TB] = jnp.where(lane // SH == k, block, 0.0).astype(LOW)
+
+    for d in range(1, nz):
+        block = dbuf.at[lax.rem(z + nz - d, nz)]
+        remote(block, block, dsend.at[d], drecv.at[d], sibling).wait_recv()
+    packed = dbuf[:, nd:lead].astype(F32).reshape(nz * nd // 2, TB)
     ddbuf[:, :nd // 2] = packed.astype(LOW).reshape(nz, nd // 2, TB)
     ddbuf[:, nd // 2:] = pltpu.roll(packed, TB - HEADS, axis=1).astype(LOW).reshape(nz, nd // 2, TB)
 
-    def backward(t, carry):
-        row, col, flag = tile_scalars(t)
-        dd = ddbuf[pl.ds(row * per, per)].reshape(TB, TB)
-        dnr = dnt[row]
-        grads = []
-        sums = []
-        for half in range(2):
-            dn = dbuf[pl.ds(row * per, per), half * nd:(half + 1) * nd].reshape(TB, TB)
-            lhs = jnp.concatenate([dn, dd], axis=1)
+    def backward(half):
+        def step(t, carry):
+            row, col, flag = tile_scalars(t)
+            dd = ddbuf[pl.ds(row * per, per)].reshape(TB, TB)
+            dn = halves[half][pl.ds(row * per, per), 0:nd].reshape(TB, TB)
             rhs = jnp.concatenate([vmaskt[t, half], onehott[half]], axis=0)
-            dsig = mm(lhs, rhs)
+            dsig = mm(jnp.concatenate([dn, dd], axis=1), rhs)
             for k in range(HALF):
                 kk = half * HALF + k
                 dl = dsig[:, k * TB:(k + 1) * TB] * gate32[t, kk]
                 gate32[t, kk] = dl
-                sums.append(jnp.sum(dl, axis=0, keepdims=True))
-                grads.append(mm(dnr[kk * SH:(kk + 1) * SH, :], gate16[t, kk]))
-        stack = jnp.concatenate(grads + sums + [jnp.zeros((TB - HEADS, TB), F32)], axis=0)
-        pt[t] = mm(stack.T.astype(LOW), wproj[...])
-        return carry
-
-    lax.fori_loop(0, slots, backward, 0, unroll=UB)
+                sums[t, kk:kk + 1] = jnp.sum(dl, axis=0, keepdims=True)
+            stack[t, :, half * TB:(half + 1) * TB] = mm(gatet[t, half], dnmask[row, half]).astype(LOW)
+            if half == 1:
+                dg = jnp.concatenate([sums[t], jnp.zeros((TB - HEADS, TB), F32)], axis=0)
+                stack[t, :, D:] = dg.T.astype(LOW)
+            return carry
+
+        lax.fori_loop(0, slots, step, 0, unroll=UB)
+
+    mask_rows(0)
+    backward(0)
+    for d in range(1, nz):
+        block = dbuf1.at[lax.rem(z + nz - d, nz)]
+        remote(block, block, d1send.at[d], d1recv.at[d], sibling).wait_recv()
+    mask_rows(1)
+    backward(1)
+    pt[:slots] = mm(stack[...].reshape(slots * TB, D + TB), wproj[...]).reshape(slots, TB, D)
 
     span = ny // cbx
     home = y // span
@@ -435,13 +449,7 @@
     own_grad = own_grad + mm(dt.astype(LOW), wtt)
     final = s2[y].astype(F32)
     for d in range(1, ny):
-        remote(ry.at[d], ry.at[d], bysend.at[d], byrecv.at[d], at_y(y)).wait_recv()
-        final += ry[d].astype(F32)
-    grad_ref[...] = own_grad + final
-
-    for d in range(1, ny):
         remote(h_ref, h_ref, ysend.at[d], yrecv.at[d], sibling).wait_send()
-        remote(s2.at[y], s2.at[y], bysend.at[d], byrecv.at[d], sibling).wait_send()
     for d in range(ny):
         for e in range(1, nx):
             remote(h_ref, h_ref, xsend.at[e, d], xrecv.at[e, d], sibling).wait_send()
@@ -456,9 +464,18 @@
         remote(send0.at[z], send0.at[z], z0send.at[d], z0recv.at[d], sibling).wait_send()
         remote(send1.at[z], send1.at[z], z1send.at[d], z1recv.at[d], sibling).wait_send()
         remote(dbuf.at[z], dbuf.at[z], dsend.at[d], drecv.at[d], sibling).wait_send()
+        remote(dbuf1.at[z], dbuf1.at[z], d1send.at[d], d1recv.at[d], sibling).wait_send()
         remote(dtsend.at[z], dtsend.at[z], gsend.at[d], grecv.at[d], sibling).wait_send()
     for t in range(slots):
         pltpu.make_async_copy(egbuf.at[t], edge_hbm.at[0, 0, t], esem.at[t]).wait()
+
+    for d in range(1, ny):
+        remote(ry.at[d], ry.at[d], bysend.at[d], byrecv.at[d], at_y(y)).wait_recv()
+        final += ry[d].astype(F32)
+    grad_ref[...] = own_grad + final
+
+    for d in range(1, ny):
+        remote(s2.at[y], s2.at[y], bysend.at[d], byrecv.at[d], sibling).wait_send()
 
 
 def flush_kernel(out_ref, grad_ref, edge_ref, out_hbm, grad_hbm, edge_hbm, out, grad, edge, isem, osem):
@@ -506,7 +523,7 @@
         pltpu.VMEM((nx, ny, 2, nd, D), LOW),
         pltpu.VMEM((nz, nd, TB), LOW),
         pltpu.VMEM((slots, HEADS, TB, TB), F32),
-        pltpu.VMEM((slots, HEADS, TB, TB), LOW),
+        pltpu.VMEM((slots, 2, TB, HALF * TB), LOW),
         pltpu.VMEM((slots, 2, HALF * TB, TB), LOW),
         pltpu.VMEM((slots, TB, D), F32),
         pltpu.VMEM((slots, 2, TB, HALF * TB), LOW),
@@ -519,9 +536,12 @@
         pltpu.VMEM((nz, nd + nd // 2, TB), LOW),
         pltpu.VMEM((nz, nd, TB), LOW),
         pltpu.VMEM((nz, nd + nd // 2, TB), LOW),
-        pltpu.VMEM((nz, 2 * nd + nd // 2, TB), LOW),
+        pltpu.VMEM((nz, nd + nd // 2, TB), LOW),
         pltpu.VMEM((nz, nd, TB), LOW),
-        pltpu.VMEM((rb, D, TB), LOW),
+        pltpu.VMEM((nz, nd, TB), LOW),
+        pltpu.VMEM((rb, 2, HALF * TB, TB), LOW),
+        pltpu.VMEM((slots, HEADS, TB), F32),
+        pltpu.VMEM((slots, TB, D + TB), LOW),
         pltpu.VMEM((slots, HEADS, TB, TB), LOW),
         pltpu.VMEM((slots + 1, TB, D), F32),
         pltpu.VMEM((D + TB, D), LOW),
@@ -539,7 +559,7 @@
         pltpu.SemaphoreType.DMA((slots,)),
     ]
     for n in (
-        (ny,), (nx, ny), (ny,), (nz,), (nz,), (nz,), (nz,), (cbx,), (nx, ny), (ny,), (nz,)
+        (ny,), (nx, ny), (ny,), (nz,), (nz,), (nz,), (nz,), (nz,), (cbx,), (nx, ny), (ny,), (nz,)
     ):
         scratch += [pltpu.SemaphoreType.DMA(n), pltpu.SemaphoreType.DMA(n)]
     shapes = (

time: 76.7 us -> 75 us (0.978)
  Pallas kernels: 75.2 us -> 73.5 us
    pallas_call x1, Pallas kernels: 72.8 us -> 71.1 us  [body(): pl.pallas_call(functools.partial(kernel, (nx, ny, nz, nd, slots)), out_sh...]
where the time goes in v4:
time: 75 us; the launch traced here: 74.8 us
  Pallas kernels  73.5 us (98%)
  between operations  1.29 us (2%)
    pallas_call x1, Pallas kernels, body(): pl.pallas_call(functools.partial(kernel, (nx, ny, nz, nd, slots)), out_sh...  71.1 us
    pallas_call x1, Pallas kernels, body(): pl.pallas_call(flush_kernel, out_shape=shapes, in_specs=[free] * 3, out_s...  2.44 us

profile of v4, /device:TPU:1, one launch (start us, length us, event | category | flops | bytes accessed | tf_op | source)
XLA Modules:
  0.0 74.8 jit_solution(7557626495242607307)
XLA Ops:
  1.3 71.1 %gated_conv.1 = (bf16[32,256]{1,0:T(8,128)(2,1)}, f32[32,256]{1,0:T(8,128)}, bf16[1,1,8,8,128,128]{5,4,3,2,1,0:T(8,128)(2,1)}) custom-call(f32[8]{0:T(128)} %scale_hbm.1, s32[1,1,2,8]{3,2,1,0:T(2,128)} %bitcast.6, s32[1,1]{1,0:T(1,128)S(6)} %copy.15.count_hbm, bf16[32,256]{1,0:T(8,128)(2,1)} %h_hbm.1, bf16[32,256]{1,0:T(8,128)(2,1)} %cot_hbm.1, ...), custom_call_target="tpu_custom_call" | custom-call | tf_op jit(solution)/shard_map/gated_conv/pallas_call | solution.py:570
  72.4 2.4 %flush.1 = (bf16[32,256]{1,0:T(8,128)(2,1)}, f32[32,256]{1,0:T(8,128)}, bf16[1,1,8,8,128,128]{5,4,3,2,1,0:T(8,128)(2,1)}) custom-call(bf16[32,256]{1,0:T(8,128)(2,1)} %get-tuple-element.6.out_ref, f32[32,256]{1,0:T(8,128)} %get-tuple-element.7.grad_ref, bf16[1,1,8,8,128,128]{5,4,3,2,1,0:T(8,128)(2,1)} %get-tuple-element.8.edge_ref), custom_call_target="tpu_custom_call" | custom-call | tf_op jit(solution)/shard_map/flush/pallas_call | solution.py:585

commit v5 on v4

--- a/solution.py
+++ b/solution.py
@@ -401,21 +401,15 @@
                     s1.at[w, v], rx.at[e, v], bxsend.at[e, i * span + j], bxrecv.at[e, i * span + j], at_x(w)
                 ).start()
 
-    def edges(t, carry):
+    def targets(t, carry):
         dt = jnp.zeros((TB, TB), F32)
         for half in range(2):
-            lows = []
-            for k in range(HALF):
-                kk = half * HALF + k
-                dl = gate32[t, kk]
-                egbuf[t, kk] = (dl * scale_ref[kk]).astype(LOW)
-                lows.append(dl.astype(LOW))
+            lows = [gate32[t, half * HALF + k].astype(LOW) for k in range(HALF)]
             dt += mm(jnp.concatenate(lows, axis=1), onehot[half])
         dtbuf[t] = dt
-        pltpu.make_async_copy(egbuf.at[t], edge_hbm.at[0, 0, t], esem.at[t]).start()
         return carry
 
-    lax.fori_loop(0, slots, edges, 0, unroll=UE)
+    lax.fori_loop(0, slots, targets, 0, unroll=UE)
     for r in range(rb):
         total = jnp.zeros((TB, TB), F32)
         for t in range(slots):
@@ -424,6 +418,14 @@
     for e in farz:
         w = lax.rem(z + e, nz)
         remote(dtsend.at[w], dtrecv.at[e], gsend.at[e], grecv.at[e], at_z(w)).start()
+
+    def edges(t, carry):
+        for k in range(HEADS):
+            egbuf[t, k] = (gate32[t, k] * scale_ref[k]).astype(LOW)
+        pltpu.make_async_copy(egbuf.at[t], edge_hbm.at[0, 0, t], esem.at[t]).start()
+        return carry
+
+    lax.fori_loop(0, slots, edges, 0, unroll=UE)
 
     for i, o in enumerate(turn):
         m = lax.rem(home + o, cbx)
@@ -480,7 +482,10 @@
 
 def flush_kernel(out_ref, grad_ref, edge_ref, out_hbm, grad_hbm, edge_hbm, out, grad, edge, isem, osem):
     slots = edge.shape[0]
-    pairs = [(edge_ref.at[0, 0, t], edge.at[t], edge_hbm.at[0, 0, t]) for t in range(slots)]
+    pairs = [
+        (edge_ref.at[0, 0, t], edge.at[t], edge_hbm.at[0, 0, t])
+        for t in (pl.ds(i, 1) for i in range(0, slots, 1))
+    ]
     pairs += [(out_ref, out, out_hbm), (grad_ref, grad, grad_hbm)]
     reads = [pltpu.make_async_copy(a, b, isem.at[i]) for i, (a, b, _) in enumerate(pairs)]
     writes = [pltpu.make_async_copy(b, c, osem.at[i]) for i, (_, b, c) in enumerate(pairs)]

time: 75 us -> 75 us (level)
  no operation moved by 1% of the time
where the time goes in v5:
time: 75 us; the launch traced here: 74.8 us
  Pallas kernels  73.5 us (98%)
  between operations  1.29 us (2%)
    pallas_call x1, Pallas kernels, body(): pl.pallas_call(functools.partial(kernel, (nx, ny, nz, nd, slots)), out_sh...  71.1 us
    pallas_call x1, Pallas kernels, body(): pl.pallas_call(flush_kernel, out_shape=shapes, in_specs=[free] * 3, out_s...  2.44 us

profile of v5, /device:TPU:1, one launch (start us, length us, event | category | flops | bytes accessed | tf_op | source)
XLA Modules:
  0.0 74.8 jit_solution(12308478141959791157)
XLA Ops:
  1.3 71.1 %gated_conv.1 = (bf16[32,256]{1,0:T(8,128)(2,1)}, f32[32,256]{1,0:T(8,128)}, bf16[1,1,8,8,128,128]{5,4,3,2,1,0:T(8,128)(2,1)}) custom-call(f32[8]{0:T(128)} %scale_hbm.1, s32[1,1,2,8]{3,2,1,0:T(2,128)} %bitcast.6, s32[1,1]{1,0:T(1,128)S(6)} %copy.15.count_hbm, bf16[32,256]{1,0:T(8,128)(2,1)} %h_hbm.1, bf16[32,256]{1,0:T(8,128)(2,1)} %cot_hbm.1, ...), custom_call_target="tpu_custom_call" | custom-call | tf_op jit(solution)/shard_map/gated_conv/pallas_call | solution.py:575
  72.4 2.4 %flush.1 = (bf16[32,256]{1,0:T(8,128)(2,1)}, f32[32,256]{1,0:T(8,128)}, bf16[1,1,8,8,128,128]{5,4,3,2,1,0:T(8,128)(2,1)}) custom-call(bf16[32,256]{1,0:T(8,128)(2,1)} %get-tuple-element.6.out_ref, f32[32,256]{1,0:T(8,128)} %get-tuple-element.7.grad_ref, bf16[1,1,8,8,128,128]{5,4,3,2,1,0:T(8,128)(2,1)} %get-tuple-element.8.edge_ref), custom_call_target="tpu_custom_call" | custom-call | tf_op jit(solution)/shard_map/flush/pallas_call | solution.py:590
